TPU v7x, 1024 devices: a whole 4x8x16 slice. The times are simulated.
1024 devices in a mesh: dp: 4 (over x), expert: 8 (over y_hi, core), tensor: 32 (over z, y_lo).
Axes of the slice: x: 4, y: 8 (y_hi: 4, y_lo: 2; y = y_hi * 2 + y_lo), z: 16, core: 2. Of those that a mesh axis runs over, the one named last changes fastest.
Arguments:
- tokens: bfloat16 [1024, 3072], P(('dp', 'expert'), 'tensor'), may hold values from -6 to 6
- expert_ids: int32 [1024, 2], P(('dp', 'expert')), may hold values from 0 to 7, all different within a row; in each aligned block of 32 rows (0 to 31, 32 to 63, ...) at most 16 rows name the same one
- gate_logits: float32 [1024, 2], P(('dp', 'expert')), may hold values from -6 to 6
- gate_weight: bfloat16 [8, 3072, 8192], P('expert', None, 'tensor'), may hold values from -0.109375 to 0.109375
- up_weight: bfloat16 [8, 3072, 8192], P('expert', None, 'tensor'), may hold values from -0.109375 to 0.109375
- down_weight: bfloat16 [8, 3072, 8192], P('expert', None, 'tensor'), may hold values from -0.0625 to 0.0625
- out_grad: bfloat16 [1024, 3072], P(('dp', 'expert'), 'tensor'), may hold values from -0.59765625 to 0.59765625
Outputs:
- mixed: bfloat16 [1024, 3072], P(('dp', 'expert'), 'tensor')
- input_grad: bfloat16 [1024, 3072], P(('dp', 'expert'), 'tensor')
- logit_grad: float32 [1024, 2], P(('dp', 'expert'))
- gate_grad: bfloat16 [8, 3072, 8192], P('expert', 'dp', 'tensor')
- up_grad: bfloat16 [8, 3072, 8192], P('expert', 'dp', 'tensor')
- down_grad: bfloat16 [8, 3072, 8192], P('expert', 'dp', 'tensor')
Inputs may be any that keep to these rules, and one draw needn't show every extreme that they name: `expert_ids`: the two experts of a token differ. Among the 32 tokens of one index of dp and expert (one device's rows), no expert is named more than 16 times, a bound that some block reaches.
All inputs are finite; a program needn't handle non-finite values.
Results may differ from a plain program's by a relative error of at most 0.035.
Values may be sent and summed in bfloat16 or wider, within the bound.
A program may use at most 64 MiB of HBM per device.

v0:
```python
import jax
import jax.numpy as jnp
from jax import lax
from jax.sharding import PartitionSpec as P


def slot_targets(expert_ids, expert_total, slot_count):
    flat_ids = expert_ids.reshape(-1)
    one_hot = (flat_ids[:, None] == jnp.arange(expert_total, dtype=jnp.int32)[None, :]).astype(
        jnp.int32
    )
    earlier = jnp.cumsum(one_hot, axis=0) - one_hot
    position = jnp.sum(earlier * one_hot, axis=1)
    return (flat_ids * slot_count + position).reshape(expert_ids.shape)


def send_out(first, second):
    return (
        lax.all_to_all(first, "expert", split_axis=0, concat_axis=0, tiled=True),
        lax.all_to_all(second, "expert", split_axis=0, concat_axis=0, tiled=True),
    )


def send_back(first, second):
    return (
        lax.all_to_all(first, "expert", split_axis=0, concat_axis=0, tiled=True),
        lax.all_to_all(second, "expert", split_axis=0, concat_axis=0, tiled=True),
    )


def widen(first, second):
    return (
        lax.all_gather(first, "tensor", axis=1, tiled=True),
        lax.all_gather(second, "tensor", axis=1, tiled=True),
    )


def on_device(tokens, expert_ids, gate_logits, gate_weight, up_weight, down_weight, out_grad):
    highest = lax.Precision.HIGHEST
    expert_total = lax.axis_size("expert")
    tok_count = tokens.shape[0]
    col_width = tokens.shape[1]
    slot_count = tok_count // 2
    row_count = expert_total * slot_count
    targets = slot_targets(expert_ids, expert_total, slot_count)
    select = (targets[:, :, None] == jnp.arange(row_count, dtype=jnp.int32)[None, None, :]).astype(
        jnp.float32
    )
    diff = gate_logits[:, 0] - gate_logits[:, 1]
    shares = jnp.stack([jax.nn.sigmoid(diff), jax.nn.sigmoid(-diff)], axis=1)
    placing = jnp.sum(select, axis=1)
    mixing = jnp.sum(select * shares[:, :, None], axis=1)
    place_half = placing.astype(jnp.bfloat16)
    w_gate = gate_weight[0]
    w_up = up_weight[0]
    w_down = down_weight[0]
    full_tokens, full_grad = widen(tokens, out_grad)
    sent = jnp.einsum(
        "tc,td->cd", place_half, full_tokens, preferred_element_type=jnp.float32
    ).astype(jnp.bfloat16)
    grad_sent = jnp.einsum(
        "tc,td->cd", mixing, full_grad.astype(jnp.float32), precision=highest
    ).astype(jnp.bfloat16)
    recv_rows, recv_grad = send_out(
        sent.reshape(expert_total, slot_count, -1), grad_sent.reshape(expert_total, slot_count, -1)
    )
    expert_rows = recv_rows.reshape(row_count, -1)
    grad_rows = recv_grad.reshape(row_count, -1)
    gate_val = jnp.dot(expert_rows, w_gate, preferred_element_type=jnp.float32)
    up_val = jnp.dot(expert_rows, w_up, preferred_element_type=jnp.float32)
    sigma = jax.nn.sigmoid(gate_val)
    active = gate_val * sigma
    hidden = (active * up_val).astype(jnp.bfloat16)
    across = (((1,), (1,)), ((), ()))
    out_term = lax.dot_general(hidden, w_down, across, preferred_element_type=jnp.float32)
    hid_grad = jnp.dot(grad_rows, w_down, preferred_element_type=jnp.float32)
    d_gate = (hid_grad * up_val * sigma * (1.0 + gate_val * (1.0 - sigma))).astype(jnp.bfloat16)
    d_up = (hid_grad * active).astype(jnp.bfloat16)
    in_term = lax.dot_general(
        d_gate, w_gate, across, preferred_element_type=jnp.float32
    ) + lax.dot_general(d_up, w_up, across, preferred_element_type=jnp.float32)
    down_rows = (((0,), (0,)), ((), ()))
    hid_width = hidden.shape[1]
    first = lax.dot_general(expert_rows, d_gate, down_rows, preferred_element_type=jnp.float32)
    second = lax.dot_general(expert_rows, d_up, down_rows, preferred_element_type=jnp.float32)
    third = lax.dot_general(grad_rows, hidden, down_rows, preferred_element_type=jnp.float32)
    weight_sums = lax.psum_scatter(
        jnp.concatenate([first, second, third], axis=1).astype(jnp.bfloat16),
        "dp",
        scatter_dimension=0,
        tiled=True,
    ).astype(jnp.float32)
    gate_grad = weight_sums[:, :hid_width].astype(jnp.bfloat16)[None]
    up_grad = weight_sums[:, hid_width : 2 * hid_width].astype(jnp.bfloat16)[None]
    down_grad = weight_sums[:, 2 * hid_width :].astype(jnp.bfloat16)[None]
    out_sum, in_sum = (
        lax.psum(out_term.astype(jnp.bfloat16), "tensor").astype(jnp.float32),
        lax.psum(in_term.astype(jnp.bfloat16), "tensor").astype(jnp.float32),
    )
    back_out, back_in = send_back(
        out_sum.astype(jnp.bfloat16).reshape(expert_total, slot_count, -1),
        in_sum.astype(jnp.bfloat16).reshape(expert_total, slot_count, -1),
    )
    back_out = back_out.reshape(row_count, -1).astype(jnp.float32)
    back_in = back_in.reshape(row_count, -1).astype(jnp.float32)
    mixed_rows = jnp.einsum("tc,cd->td", mixing, back_out, precision=highest)
    input_rows = jnp.einsum("tc,cd->td", placing, back_in, precision=highest)
    inner = jnp.einsum("td,cd->tc", full_grad.astype(jnp.float32), back_out, precision=highest)
    weighted = jnp.sum(select * inner[:, None, :], axis=2)
    col_start = lax.axis_index("tensor") * col_width
    mixed = lax.dynamic_slice_in_dim(mixed_rows, col_start, col_width, 1)
    input_grad = lax.dynamic_slice_in_dim(input_rows, col_start, col_width, 1)
    logit_grad = shares * (weighted - jnp.sum(shares * weighted, axis=1, keepdims=True))
    return (
        mixed.astype(jnp.bfloat16),
        input_grad.astype(jnp.bfloat16),
        logit_grad,
        gate_grad,
        up_grad,
        down_grad,
    )


def solution(mesh):
    return jax.shard_map(
        on_device,
        mesh=mesh,
        in_specs=(
            P(("dp", "expert"), "tensor"),
            P(("dp", "expert"), None),
            P(("dp", "expert"), None),
            P("expert", None, "tensor"),
            P("expert", None, "tensor"),
            P("expert", None, "tensor"),
            P(("dp", "expert"), "tensor"),
        ),
        out_specs=(
            P(("dp", "expert"), "tensor"),
            P(("dp", "expert"), "tensor"),
            P(("dp", "expert"), None),
            P("expert", "dp", "tensor"),
            P("expert", "dp", "tensor"),
            P("expert", "dp", "tensor"),
        ),
        check_vma=False,
    )
```

profile of v0, /device:TPU:1, one launch (start us, length us, event | category | flops | bytes accessed | tf_op | source)
XLA Modules:
  0.0 842.0 jit_solution(7689980927998699827)
XLA Ops:
  7.2 64.3 %all-gather = bf16[32,96,32]{1,2,0:T(8,128)(2,1)S(1)} all-gather(bf16[1,96,32]{1,2,0:T(8,128)(2,1)} %bitcast.79), channel_id=1, replica_groups=mesh['dp'=4,'expert'=8,'tensor'=32] {'tensor'}, dimensions={0}, use_global_device_ids=true | all-gather | bytes 202752 | tf_op jit(solution)/shard_map/all_gather | solution.py:33
  74.6 41.8 %all_to_all.20 = bf16[8,16,3072]{2,1,0:T(8,128)(2,1)S(1)} all-to-all(bf16[8,16,3072]{2,1,0:T(8,128)(2,1)S(1)} %bitcast.73), channel_id=1, replica_groups=mesh['dp'=4,'expert'=8,'tensor'=32] {'expert'}, dimensions={0} | all-to-all | bytes 1572864 | tf_op jit(solution)/shard_map/all_to_all | solution.py:19
  116.5 1.9 fusion.9
  118.4 1.0 multiply_convert_fusion.2
  119.4 1.5 convolution_convert_fusion.5
  121.0 238.5 %all-reduce.3.cloned.1.call-done = bf16[8,16,3072]{2,1,0:T(8,128)(2,1)} async-done(((bf16[8,16,3072]{2,1,0:T(8,128)(2,1)}), bf16[8,16,3072]{2,1,0:T(8,128)(2,1)}) %all-reduce.3.cloned.1.call-update) | async-done | bytes 786448 | tf_op jit(solution)/shard_map/psum | solution.py:97
  359.5 28.8 %all-to-all-start.1 = ((bf16[8,16,3072]{2,1,0:T(8,128)(2,1)}), bf16[8,16,3072]{2,1,0:T(8,128)(2,1)S(1)}, u32[]{:S(2)}, u32[]{:S(2)}) async-start(bf16[8,16,3072]{2,1,0:T(8,128)(2,1)} %all-reduce.3.cloned.1.call-done), calls=%async_computation.1 | async-start | bytes 1572864 | tf_op jit(solution)/shard_map/all_to_all | solution.py:26
  388.3 59.3 %all-gather.1 = bf16[32,96,32]{1,2,0:T(8,128)(2,1)S(1)} all-gather(bf16[1,96,32]{1,2,0:T(8,128)(2,1)S(1)} %bitcast.80), channel_id=1, replica_groups=mesh['dp'=4,'expert'=8,'tensor'=32] {'tensor'}, dimensions={0}, use_global_device_ids=true | all-gather | bytes 202752 | tf_op jit(solution)/shard_map/all_gather | solution.py:34
  448.4 1.3 reshape.58
  451.9 1.4 select_reduce_fusion
  453.3 0.8 convolution_convert_fusion.3
  454.2 44.2 %all_to_all.21 = bf16[8,16,3072]{2,1,0:T(8,128)(2,1)S(1)} all-to-all(bf16[8,16,3072]{2,1,0:T(8,128)(2,1)S(1)} %bitcast.74), channel_id=1, replica_groups=mesh['dp'=4,'expert'=8,'tensor'=32] {'expert'}, dimensions={0} | all-to-all | bytes 1572864 | tf_op jit(solution)/shard_map/all_to_all | solution.py:20
  498.4 1.8 convolution_convert_fusion
  500.5 1.0 copy-done.1
  502.9 1.5 fusion
  506.6 2.4 pad_maximum_fusion
  509.1 238.2 %all-reduce.5.cloned.1.call-done = bf16[8,16,3072]{2,1,0:T(8,128)(2,1)} async-done(((bf16[8,16,3072]{2,1,0:T(8,128)(2,1)}), bf16[8,16,3072]{2,1,0:T(8,128)(2,1)}) %all-reduce.5.cloned.1.call-update) | async-done | bytes 786448 | tf_op jit(solution)/shard_map/psum | solution.py:98
  747.2 28.2 %all-to-all-start.3 = ((bf16[8,16,3072]{2,1,0:T(8,128)(2,1)}), bf16[8,16,3072]{2,1,0:T(8,128)(2,1)S(1)}, u32[]{:S(2)}, u32[]{:S(2)}) async-start(bf16[8,16,3072]{2,1,0:T(8,128)(2,1)} %all-reduce.5.cloned.1.call-done), calls=%async_computation.3 | async-start | bytes 1572864 | tf_op jit(solution)/shard_map/all_to_all | solution.py:27
  777.2 18.9 %all-to-all-done.3 = bf16[8,16,3072]{2,1,0:T(8,128)(2,1)S(1)} async-done(((bf16[8,16,3072]{2,1,0:T(8,128)(2,1)}), bf16[8,16,3072]{2,1,0:T(8,128)(2,1)S(1)}, u32[]{:S(2)}, u32[]{:S(2)}) %all-to-all-start.3) | async-done | bytes 786464 | tf_op jit(solution)/shard_map/all_to_all | solution.py:27
  797.2 34.2 %reduce-scatter.2.cloned.1.call-done = bf16[768,768]{0,1:T(8,128)(2,1)} async-done(((bf16[3072,768]{0,1:T(8,128)(2,1)}), bf16[768,768]{0,1:T(8,128)(2,1)}) %reduce-scatter.2.cloned.1.call-update) | async-done | bytes 1179664 | tf_op jit(solution)/shard_map/reduce_scatter | solution.py:87
  831.4 1.3 slice_bitcast_fusion
  832.7 0.9 copy.51
  833.7 0.9 copy.52
  834.6 0.9 copy.53
  (62 shorter events, 12.9 us)
Async XLA Ops:
  7.2 112.2 %copy-start = (bf16[1,3072,256]{2,1,0:T(8,128)(2,1)S(1)}, bf16[1,3072,256]{2,1,0:T(8,128)(2,1)}, u32[]{:S(2)}) copy-start(bf16[1,3072,256]{2,1,0:T(8,128)(2,1)} %param.12) | copy-start | bytes 4718596
  7.2 352.3 %all-reduce.3.cloned.1.call-start = ((), (), s32[]{:S(2)}) async-start(), calls=%async_computation.5 | async-start | bytes 1572864 | tf_op jit(solution)/shard_map/psum | solution.py:97
  74.0 0.6 copy-start.8
  116.5 1.9 copy-start.3
  120.9 267.3 %copy-start.10 = (bf16[32,96]{1,0:T(8,128)(2,1)S(1)}, bf16[32,96]{1,0:T(8,128)(2,1)}, u32[]{:S(2)}) copy-start(bf16[32,96]{1,0:T(8,128)(2,1)} %param.13) | copy-start | bytes 18436
  359.5 92.0 %all-to-all-start.1 = ((bf16[8,16,3072]{2,1,0:T(8,128)(2,1)}), bf16[8,16,3072]{2,1,0:T(8,128)(2,1)S(1)}, u32[]{:S(2)}, u32[]{:S(2)}) async-start(bf16[8,16,3072]{2,1,0:T(8,128)(2,1)} %all-reduce.3.cloned.1.call-done), calls=%async_computation.1 | async-start | bytes 1572864 | tf_op jit(solution)/shard_map/all_to_all | solution.py:26
  388.3 359.0 %all-reduce.5.cloned.1.call-start = ((), (), s32[]{:S(2)}) async-start(), calls=%async_computation.6 | async-start | bytes 1572864 | tf_op jit(solution)/shard_map/psum | solution.py:98
  450.4 0.5 copy-start.11
  450.4 0.5 copy-start.13
  453.3 45.0 %copy-start.5 = (f32[32,128]{1,0:T(8,128)}, f32[32,128]{1,0:T(8,128)S(1)}, u32[]{:S(2)}) copy-start(f32[32,128]{1,0:T(8,128)S(1)} %get-tuple-element.37) | copy-start | bytes 49156
  498.4 1.8 copy-start.7
  500.1 1.4 copy-start.1
  501.5 1.4 copy-start.4
  504.5 326.9 %reduce-scatter.2.cloned.1.call-start = ((), (), s32[]{:S(2)}) async-start(), calls=%async_computation.7 | async-start | bytes 5898240 | tf_op jit(solution)/shard_map/reduce_scatter | solution.py:87
  505.2 1.4 copy-start.2
  509.0 266.5 %copy-start.9 = (f32[32,2]{0,1:T(2,128)S(1)}, f32[32,2]{0,1:T(2,128)}, u32[]{:S(2)}) copy-start(f32[32,2]{0,1:T(2,128)} %get-tuple-element.36) | copy-start | bytes 772
  509.0 266.4 %copy-start.12 = (f32[32,1]{0,1:T(1,128)S(1)}, f32[32,1]{0,1:T(1,128)}, u32[]{:S(2)}) copy-start(f32[32,1]{0,1:T(1,128)} %copy-done.11) | copy-start | bytes 388
  509.0 266.4 %copy-start.14 = (f32[32,1]{0,1:T(1,128)S(1)}, f32[32,1]{0,1:T(1,128)}, u32[]{:S(2)}) copy-start(f32[32,1]{0,1:T(1,128)} %copy-done.13) | copy-start | bytes 388
  509.0 266.5 %copy-start.6 = (f32[32,128]{1,0:T(8,128)S(1)}, f32[32,128]{1,0:T(8,128)}, u32[]{:S(2)}) copy-start(f32[32,128]{1,0:T(8,128)} %copy-done.5) | copy-start | bytes 49156
  747.2 48.9 %all-to-all-start.3 = ((bf16[8,16,3072]{2,1,0:T(8,128)(2,1)}), bf16[8,16,3072]{2,1,0:T(8,128)(2,1)S(1)}, u32[]{:S(2)}, u32[]{:S(2)}) async-start(bf16[8,16,3072]{2,1,0:T(8,128)(2,1)} %all-reduce.5.cloned.1.call-done), calls=%async_computation.3 | async-start | bytes 1572864 | tf_op jit(solution)/shard_map/all_to_all | solution.py:27
Sparse Core Ops, SparseCore 0:
  121.1 238.3 all-reduce.2
  504.6 242.5 all-reduce.4
  750.7 80.6 reduce-scatter.1
where the time goes:
time: 843 us; the launch traced here: 842 us
  waiting for transfers between devices  530 us (63%)
  blocking collectives  210 us (25%)
  starting transfers between devices  57.1 us (7%)
  between operations  13.9 us (2%)
  matrix products  12.5 us (1%)
  local copies, waits for them, and re-layouts  12.2 us (1%)
    psum x1, waiting for transfers between devices, on_device(): lax.psum(out_term.astype(jnp.bfloat16), 'tensor').astype(jnp.float32)  239 us
    psum x1, waiting for transfers between devices, on_device(): lax.psum(in_term.astype(jnp.bfloat16), 'tensor').astype(jnp.float32)  238 us
    all_gather x1, blocking collectives, widen(): lax.all_gather(first, 'tensor', axis=1, tiled=True)  64.3 us
    all_gather x1, blocking collectives, widen(): lax.all_gather(second, 'tensor', axis=1, tiled=True)  59.3 us
    all_to_all x1, blocking collectives, send_out(): lax.all_to_all(second, 'expert', split_axis=0, concat_axis=0, tiled=True)  44.2 us
    all_to_all x1, blocking collectives, send_out(): lax.all_to_all(first, 'expert', split_axis=0, concat_axis=0, tiled=True)  41.8 us
    reduce_scatter x1, waiting for transfers between devices, on_device(): lax.psum_scatter(jnp.concatenate([first, second, third], axis=1).astype(j...  34.2 us
    all_to_all x1, starting transfers between devices, send_back(): lax.all_to_all(first, 'expert', split_axis=0, concat_axis=0, tiled=True)  28.8 us
  transfers between devices with their start and end apart: 5, of which 4 were waited for; matrix products, arithmetic and copies ran while one was open for 1% of the time, Pallas kernels for 0%

commit v1 on v0

v1 whole, which is shorter than its diff:
```python
import functools

import jax
import jax.numpy as jnp
from jax import lax
from jax.experimental import pallas as pl
from jax.experimental.pallas import tpu as pltpu
from jax.sharding import PartitionSpec as P

MESH = pl.DeviceIdType.MESH
F32 = jnp.float32
BF16 = jnp.bfloat16
Y = 2


def dot(a, b):
    return jnp.dot(a, b, preferred_element_type=F32)


def dot_tn(a, b):
    return lax.dot_general(a, b, (((0,), (0,)), ((), ())), preferred_element_type=F32)


def dot_nt(a, b, precision=None):
    return lax.dot_general(
        a, b, (((1,), (1,)), ((), ())), precision=precision, preferred_element_type=F32
    )


def eye(n):
    rows = lax.broadcasted_iota(jnp.int32, (n, n), 0)
    cols = lax.broadcasted_iota(jnp.int32, (n, n), 1)
    return (rows == cols).astype(F32).astype(BF16)


def kernel(
    sizes,
    tok_ref,
    ids_ref,
    logit_ref,
    wg_hbm,
    wu_hbm,
    wd_hbm,
    og_ref,
    mixed_ref,
    in_grad_ref,
    logit_grad_ref,
    gate_grad_ref,
    up_grad_ref,
    down_grad_ref,
    wg,
    wu,
    wd,
    stage,
    out0,
    in0,
    xg,
    acc,
    both_sums,
    hid,
    xq,
    hq,
    plus_out,
    plus_in,
    minus_out,
    minus_in,
    pair_out,
    pair_in,
    sw_out,
    sw_in,
    sw_all,
    out4,
    in4,
    w_sem,
    s0_sem,
    r0_sem,
    sy_sem,
    ry_sem,
    sp_sem,
    rp_sem,
    sm_sem,
    rm_sem,
    xq_s,
    xq_r,
    hq_s,
    hq_r,
    tp_s,
    tp_r,
    tm_s,
    tm_r,
    pair_s,
    pair_r,
    sw_s,
    sw_r,
    swx_s,
    swx_r,
    s4_sem,
    r4_sem,
):
    n_dp, n_exp, nz, tok, feat, hidw, pad = sizes
    slot = tok // 2
    rows = n_exp * slot
    hp, hm = nz // 2, nz // 2 - 1
    planes = nz // n_dp
    d = lax.axis_index("dp")
    e = lax.axis_index("expert")
    t_me = lax.axis_index("tensor")
    z, y = t_me // Y, t_me % Y
    y_other = 1 - y
    up_to = lax.rem(z + 1, nz) * Y + y
    down_to = lax.rem(z + nz - 1, nz) * Y + y
    pair = z * Y + y_other
    strides = []
    m = 1
    while m < nz:
        strides.append(m)
        m *= 2

    def flip(m):
        return (z + m - 2 * m * (lax.rem(z // m, 2))) * Y + y

    tensor_peers = [up_to, down_to, pair] + [
        flip(m) for m in strides if m not in (1, nz - 1)
    ]
    barrier = pltpu.get_barrier_semaphore()
    for peer in tensor_peers:
        pl.semaphore_signal(barrier, inc=1, device_id={"tensor": peer}, device_id_type=MESH)
    for o in range(1, n_exp):
        pl.semaphore_signal(
            barrier, inc=1, device_id={"expert": lax.rem(e + o, n_exp)}, device_id_type=MESH
        )
    for o in range(1, n_dp):
        pl.semaphore_signal(
            barrier, inc=1, device_id={"dp": lax.rem(d + o, n_dp)}, device_id_type=MESH
        )
    loads = [
        pltpu.make_async_copy(src, dst, w_sem.at[i])
        for i, (src, dst) in enumerate(((wg_hbm, wg), (wu_hbm, wu), (wd_hbm, wd)))
    ]
    for load in loads:
        load.start()

    ids = ids_ref[...]
    id_k = (ids[:, 0:1], ids[:, 1:2])
    lanes = lax.broadcasted_iota(jnp.int32, (tok, 128), 1)
    hot = [(lanes == i).astype(F32) for i in id_k]
    later = lax.broadcasted_iota(jnp.int32, (tok, tok), 0)
    earlier = lax.broadcasted_iota(jnp.int32, (tok, tok), 1)
    before = (earlier < later).astype(F32).astype(BF16)
    count = dot(before, (hot[0] + hot[1]).astype(BF16))
    place = [jnp.sum(h * count, axis=1, keepdims=True).astype(jnp.int32) for h in hot]
    row_lane = lax.broadcasted_iota(jnp.int32, (tok, rows), 1)
    select = [
        (row_lane == i * slot + p).astype(F32).astype(BF16) for i, p in zip(id_k, place)
    ]
    logits = logit_ref[...]
    diff = logits[:, 0:1] - logits[:, 1:2]
    share = (jax.nn.sigmoid(diff), jax.nn.sigmoid(-diff))

    stage[...] = jnp.zeros_like(stage)
    out4[...] = jnp.zeros_like(out4)
    tokens = tok_ref[...]
    grads = og_ref[...].astype(F32)
    for k in range(2):
        stage[k * tok : (k + 1) * tok, 0:feat] = tokens
        stage[k * tok : (k + 1) * tok, pad : pad + feat] = (share[k] * grads).astype(BF16)
    placed = dot_tn(jnp.concatenate(select, axis=0), stage[...]).astype(BF16)
    out0[...] = placed.reshape(n_exp, slot, 2 * pad)

    pl.semaphore_wait(barrier, len(tensor_peers) + n_exp - 1 + n_dp - 1)

    def swap(src, dst, send, recv, o):
        return pltpu.make_async_remote_copy(
            src_ref=src.at[lax.rem(e + o, n_exp)],
            dst_ref=dst.at[e],
            send_sem=send.at[o - 1],
            recv_sem=recv.at[o - 1],
            device_id={"expert": lax.rem(e + o, n_exp)},
            device_id_type=MESH,
        )

    for o in range(1, n_exp):
        swap(out0, in0, s0_sem, r0_sem, o).start()
    in0[pl.ds(e, 1)] = out0[pl.ds(e, 1)]
    for o in range(1, n_exp):
        swap(out0, in0, s0_sem, r0_sem, o).wait_recv()

    unit = eye(pad)
    for a in range(2):
        arrived = in0[:, :, a * pad : (a + 1) * pad].reshape(rows, pad)
        turned = dot_nt(unit, arrived)
        xg[pl.ds(z, 1), pl.ds(y, 1), a] = turned[0:feat].astype(BF16)[None, None]

    def to_pair():
        return pltpu.make_async_remote_copy(
            src_ref=xg.at[z, y],
            dst_ref=xg.at[z, y],
            send_sem=sy_sem,
            recv_sem=ry_sem,
            device_id={"tensor": pair},
            device_id_type=MESH,
        )

    def hop(up, k, c):
        block = lax.rem(z - k + nz, nz) if up else lax.rem(z + k, nz)
        half = y if c == 0 else y_other
        return pltpu.make_async_remote_copy(
            src_ref=xg.at[block, half],
            dst_ref=xg.at[block, half],
            send_sem=(sp_sem if up else sm_sem).at[k, c],
            recv_sem=(rp_sem if up else rm_sem).at[k, c],
            device_id={"tensor": up_to if up else down_to},
            device_id_type=MESH,
        )

    def accumulate(block):
        both = xg[pl.ds(block, 1)]
        xt = both[0, :, 0].reshape(Y * feat, rows)
        gt = both[0, :, 1].reshape(Y * feat, rows)
        acc[0] += dot_tn(xt, wg[pl.ds(block, 1)][0])
        acc[1] += dot_tn(xt, wu[pl.ds(block, 1)][0])
        acc[2] += dot_tn(gt, wd[pl.ds(block, 1)][0])

    to_pair().start()
    hop(True, 0, 0).start()
    if hm > 0:
        hop(False, 0, 0).start()
    acc[...] = jnp.zeros_like(acc)
    for load in loads:
        load.wait()
    to_pair().wait_recv()
    hop(True, 0, 1).start()
    if hm > 0:
        hop(False, 0, 1).start()
    accumulate(z)

    @pl.loop(1, max(hm, 1))
    def _(k):
        for c in range(2):
            hop(True, k - 1, c).wait_recv()
            hop(True, k, c).start()
            hop(False, k - 1, c).wait_recv()
            hop(False, k, c).start()
        accumulate(lax.rem(z - k + nz, nz))
        accumulate(lax.rem(z + k, nz))

    if hm > 0:
        for c in range(2):
            hop(True, hp - 2, c).wait_recv()
            hop(True, hp - 1, c).start()
        for c in range(2):
            hop(False, hm - 1, c).wait_recv()
        accumulate(lax.rem(z - hm + nz, nz))
        accumulate(lax.rem(z + hm, nz))
    for c in range(2):
        hop(True, hp - 1, c).wait_recv()
    accumulate(lax.rem(z - hp + nz, nz))

    def quarter(o):
        peer = lax.rem(d + o, n_dp)
        return pltpu.make_async_remote_copy(
            src_ref=xg.at[pl.ds(peer * planes, planes)],
            dst_ref=xq.at[o - 1],
            send_sem=xq_s.at[o - 1],
            recv_sem=xq_r.at[o - 1],
            device_id={"dp": peer},
            device_id_type=MESH,
        )

    def factors(o):
        return pltpu.make_async_remote_copy(
            src_ref=hid,
            dst_ref=hq.at[o - 1],
            send_sem=hq_s.at[o - 1],
            recv_sem=hq_r.at[o - 1],
            device_id={"dp": lax.rem(d + o, n_dp)},
            device_id_type=MESH,
        )

    for o in range(1, n_dp):
        quarter(o).start()

    gate, lift, hid_grad = acc[0], acc[1], acc[2]
    sigma = jax.nn.sigmoid(gate)
    active = gate * sigma
    hidden = active * lift
    hid[:, 0:hidw] = hidden.astype(BF16)
    hid[:, hidw : 2 * hidw] = (
        hid_grad * lift * sigma * (1.0 + gate * (1.0 - sigma))
    ).astype(BF16)
    hid[:, 2 * hidw : 3 * hidw] = (hid_grad * active).astype(BF16)

    def own(block, a):
        if a == 0:
            return dot_nt(wd[pl.ds(block, 1)][0], hid[:, 0:hidw])
        return dot_nt(wg[pl.ds(block, 1)][0], hid[:, hidw : 2 * hidw]) + dot_nt(
            wu[pl.ds(block, 1)][0], hid[:, 2 * hidw : 3 * hidw]
        )

    def pass_on(up, k, a):
        return pltpu.make_async_remote_copy(
            src_ref=(plus_out if up else minus_out).at[k, a],
            dst_ref=(plus_in if up else minus_in).at[k, a],
            send_sem=(tp_s if up else tm_s).at[k, a],
            recv_sem=(tp_r if up else tm_r).at[k, a],
            device_id={"tensor": up_to if up else down_to},
            device_id_type=MESH,
        )

    def taken(up, k, a):
        pass_on(up, k, a).wait_recv()
        got = (plus_in if up else minus_in)[pl.ds(k, 1), a]
        return got.reshape(Y * feat, rows).astype(F32)

    def reduce_step(k, first, ways):
        for a in range(2):
            for up in ways:
                block = lax.rem(z + hp - k, nz) if up else lax.rem(z - hm + k + nz, nz)
                term = own(block, a)
                if not first:
                    term = term + taken(up, k - 1, a)
                buf = plus_out if up else minus_out
                buf[pl.ds(k, 1), a] = term.astype(BF16).reshape(1, Y, feat, rows)
                pass_on(up, k, a).start()

    def sw_copy(i, peer):
        return pltpu.make_async_remote_copy(
            src_ref=sw_out.at[i],
            dst_ref=sw_in.at[i],
            send_sem=sw_s.at[i],
            recv_sem=sw_r.at[i],
            device_id={"tensor": peer},
            device_id_type=MESH,
        )

    def sw_stage(i, m):
        sw_copy(i - 1, pair).wait_recv()
        sw_out[pl.ds(i, 1)] = sw_out[pl.ds(i - 1, 1)] + sw_in[pl.ds(i - 1, 1)]
        sw_copy(i, flip(m)).start()
        return 2 * m

    ways = (True, False) if hm > 0 else (True,)
    reduce_step(0, True, ways)
    for o in range(1, n_dp):
        factors(o).start()
    sw_out[0] = dot_nt(
        jnp.ones((8, hidw), F32), hidden * hid_grad, lax.Precision.HIGHEST
    )
    sw_copy(0, pair).start()

    n_mid = max(hm - 1, 0)
    with_sw = min(n_mid, len(strides))

    def early(k, m):
        reduce_step(k, False, ways)
        return sw_stage(k, m)

    def late(k, m):
        reduce_step(k, False, ways)
        return m

    m = lax.fori_loop(1, 1 + with_sw, early, jnp.int32(1))
    lax.fori_loop(1 + with_sw, 1 + n_mid, late, jnp.int32(1))
    for i in range(with_sw, len(strides)):
        m = sw_stage(i + 1, m)
    last = len(strides)
    sw_copy(last, pair).wait_recv()
    sw_all[pl.ds(e, 1)] = (sw_out[last] + sw_in[last])[None]

    def sw_swap(o):
        return pltpu.make_async_remote_copy(
            src_ref=sw_all.at[e],
            dst_ref=sw_all.at[e],
            send_sem=swx_s.at[o - 1],
            recv_sem=swx_r.at[o - 1],
            device_id={"expert": lax.rem(e + o, n_exp)},
            device_id_type=MESH,
        )

    for o in range(1, n_exp):
        sw_swap(o).start()
    if hm > 0:
        reduce_step(hp - 1, False, (True,))

    def halves(a):
        term = own(z, a) + taken(True, hp - 1, a)
        if hm > 0:
            term = term + taken(False, hm - 1, a)
        both_sums[a] = term.reshape(Y, feat, rows)

    def to_partner(a):
        return pltpu.make_async_remote_copy(
            src_ref=pair_out.at[a],
            dst_ref=pair_in.at[a],
            send_sem=pair_s.at[a],
            recv_sem=pair_r.at[a],
            device_id={"tensor": pair},
            device_id_type=MESH,
        )

    for a in range(2):
        halves(a)
        pair_out[a] = both_sums[a, pl.ds(y_other, 1)][0].astype(BF16)
        to_partner(a).start()
    back = eye(rows)
    for a in range(2):
        mine = both_sums[a, pl.ds(y, 1)][0]
        to_partner(a).wait_recv()
        total = (mine + pair_in[a].astype(F32)).astype(BF16)
        turned = dot_nt(back, total).astype(BF16)
        out4[:, :, a * pad : a * pad + feat] = turned.reshape(n_exp, slot, feat)
    for o in range(1, n_exp):
        swap(out4, in4, s4_sem, r4_sem, o).start()
    in4[pl.ds(e, 1)] = out4[pl.ds(e, 1)]

    for o in range(1, n_dp):
        quarter(o).wait_recv()
        factors(o).wait_recv()

    @pl.loop(0, planes)
    def _(p):
        both = [xg[pl.ds(d * planes + p, 1)][0]] + [
            xq[o, pl.ds(p, 1)][0] for o in range(n_dp - 1)
        ]
        parts = [hid] + [hq.at[o] for o in range(n_dp - 1)]
        here = pl.ds(pl.multiple_of(p * Y * feat, Y * feat), Y * feat)
        for ref, a, i in (
            (gate_grad_ref, 0, 1),
            (up_grad_ref, 0, 2),
            (down_grad_ref, 1, 0),
        ):
            total = None
            for b, h in zip(both, parts):
                term = dot(b[:, a].reshape(Y * feat, rows), h[:, i * hidw : (i + 1) * hidw])
                total = term if total is None else total + term
            ref[here, :] = total.astype(BF16)

    for o in range(1, n_exp):
        swap(out4, in4, s4_sem, r4_sem, o).wait_recv()
        sw_swap(o).wait_recv()
    came = in4[...].reshape(rows, 2 * pad)
    picked = [dot(s, came) for s in select]
    mixed_ref[...] = (
        share[0] * picked[0][:, 0:feat] + share[1] * picked[1][:, 0:feat]
    ).astype(BF16)
    in_grad_ref[...] = (
        picked[0][:, pad : pad + feat] + picked[1][:, pad : pad + feat]
    ).astype(BF16)
    sw_lane = lax.broadcasted_iota(jnp.int32, (tok, rows), 1)
    sw = []
    for k in range(2):
        line = jnp.zeros((tok, rows), F32)
        for i in range(n_exp):
            line = line + hot[k][:, i : i + 1] * jnp.concatenate([sw_all[i]] * (tok // 8), axis=0)
        here = sw_lane == e * slot + place[k]
        sw.append(jnp.sum(jnp.where(here, line, 0.0), axis=1, keepdims=True))
    first = share[1] * sw[0] - share[0] * sw[1]
    column = lax.broadcasted_iota(jnp.int32, (tok, 2), 1)
    logit_grad_ref[...] = jnp.where(column == 0, first, -first)

    for o in range(1, n_exp):
        swap(out0, in0, s0_sem, r0_sem, o).wait_send()
        swap(out4, in4, s4_sem, r4_sem, o).wait_send()
        sw_swap(o).wait_send()
    to_pair().wait_send()
    for o in range(1, n_dp):
        quarter(o).wait_send()
        factors(o).wait_send()
    for i in range(len(strides) + 1):
        sw_copy(i, pair).wait_send()
    for a in range(2):
        to_partner(a).wait_send()

    @pl.loop(0, hp)
    def _(k):
        for c in range(2):
            hop(True, k, c).wait_send()
            pass_on(True, k, c).wait_send()

    @pl.loop(0, hm)
    def _(k):
        for c in range(2):
            hop(False, k, c).wait_send()
            pass_on(False, k, c).wait_send()


def solution(mesh):
    n_dp, n_exp, n_t = mesh.shape["dp"], mesh.shape["expert"], mesh.shape["tensor"]
    nz = n_t // Y

    def on_device(tokens, expert_ids, gate_logits, gate_weight, up_weight, down_weight, out_grad):
        tok, feat = tokens.shape
        hidw = gate_weight.shape[2]
        slot = tok // 2
        rows = n_exp * slot
        hp, hm = nz // 2, nz // 2 - 1
        hmb = max(hm, 1)
        planes = nz // n_dp
        pad = -(-feat // 128) * 128
        stages = nz.bit_length()
        width = feat * n_t // n_dp
        vmem = pl.BlockSpec(memory_space=pltpu.VMEM)
        hbm = pl.BlockSpec(memory_space=pl.ANY)
        dma = pltpu.SemaphoreType.DMA
        weights = [w.reshape(nz, Y * feat, hidw) for w in (gate_weight, up_weight, down_weight)]
        grad = jax.ShapeDtypeStruct((width, hidw), BF16)
        outs = pl.pallas_call(
            functools.partial(kernel, (n_dp, n_exp, nz, tok, feat, hidw, pad)),
            out_shape=(
                jax.ShapeDtypeStruct((tok, feat), BF16),
                jax.ShapeDtypeStruct((tok, feat), BF16),
                jax.ShapeDtypeStruct((tok, 2), F32),
                grad,
                grad,
                grad,
            ),
            in_specs=[vmem, vmem, vmem, hbm, hbm, hbm, vmem],
            out_specs=[vmem] * 6,
            scratch_shapes=[
                pltpu.VMEM((nz, Y * feat, hidw), BF16),
                pltpu.VMEM((nz, Y * feat, hidw), BF16),
                pltpu.VMEM((nz, Y * feat, hidw), BF16),
                pltpu.VMEM((2 * tok, 2 * pad), BF16),
                pltpu.VMEM((n_exp, slot, 2 * pad), BF16),
                pltpu.VMEM((n_exp, slot, 2 * pad), BF16),
                pltpu.VMEM((nz, Y, 2, feat, rows), BF16),
                pltpu.VMEM((3, rows, hidw), F32),
                pltpu.VMEM((2, Y, feat, rows), F32),
                pltpu.VMEM((rows, 3 * hidw), BF16),
                pltpu.VMEM((n_dp - 1, planes, Y, 2, feat, rows), BF16),
                pltpu.VMEM((n_dp - 1, rows, 3 * hidw), BF16),
                pltpu.VMEM((hp, 2, Y, feat, rows), BF16),
                pltpu.VMEM((hp, 2, Y, feat, rows), BF16),
                pltpu.VMEM((hmb, 2, Y, feat, rows), BF16),
                pltpu.VMEM((hmb, 2, Y, feat, rows), BF16),
                pltpu.VMEM((2, feat, rows), BF16),
                pltpu.VMEM((2, feat, rows), BF16),
                pltpu.VMEM((stages, 8, rows), F32),
                pltpu.VMEM((stages, 8, rows), F32),
                pltpu.VMEM((n_exp, 8, rows), F32),
                pltpu.VMEM((n_exp, slot, 2 * pad), BF16),
                pltpu.VMEM((n_exp, slot, 2 * pad), BF16),
                dma((3,)),
                dma((n_exp - 1,)),
                dma((n_exp - 1,)),
                dma,
                dma,
                dma((hp, 2)),
                dma((hp, 2)),
                dma((hmb, 2)),
                dma((hmb, 2)),
                dma((n_dp - 1,)),
                dma((n_dp - 1,)),
                dma((n_dp - 1,)),
                dma((n_dp - 1,)),
                dma((hp, 2)),
                dma((hp, 2)),
                dma((hmb, 2)),
                dma((hmb, 2)),
                dma((2,)),
                dma((2,)),
                dma((stages,)),
                dma((stages,)),
                dma((n_exp - 1,)),
                dma((n_exp - 1,)),
                dma((n_exp - 1,)),
                dma((n_exp - 1,)),
            ],
            compiler_params=pltpu.CompilerParams(
                collective_id=0, has_side_effects=True, vmem_limit_bytes=40 * 1024 * 1024
            ),
        )(tokens, expert_ids, gate_logits, *weights, out_grad)
        mixed, in_grad, logit_grad, gate_grad, up_grad, down_grad = outs
        return mixed, in_grad, logit_grad, gate_grad[None], up_grad[None], down_grad[None]

    return jax.shard_map(
        on_device,
        mesh=mesh,
        in_specs=(
            P(("dp", "expert"), "tensor"),
            P(("dp", "expert"), None),
            P(("dp", "expert"), None),
            P("expert", None, "tensor"),
            P("expert", None, "tensor"),
            P("expert", None, "tensor"),
            P(("dp", "expert"), "tensor"),
        ),
        out_specs=(
            P(("dp", "expert"), "tensor"),
            P(("dp", "expert"), "tensor"),
            P(("dp", "expert"), None),
            P("expert", "dp", "tensor"),
            P("expert", "dp", "tensor"),
            P("expert", "dp", "tensor"),
        ),
        check_vma=False,
    )
```

time: 843 us -> 111 us (0.13)
  waiting for transfers between devices: 530 us -> 0 us
  blocking collectives: 210 us -> 0 us
  Pallas kernels: 0 us -> 98.8 us
  starting transfers between devices: 57.1 us -> 0 us
  between operations: 13.9 us -> 0.65 us
  matrix products: 12.5 us -> 0 us
    psum x2 -> x0, waiting for transfers between devices: 477 us -> none  [the longest x1 239 us: on_device(): lax.psum(out_term.astype(jnp.bfloat16), 'tensor').astype(jnp.float32)]
    all_gather x2 -> x0, blocking collectives: 124 us -> none  [the longest x1 64.3 us: widen(): lax.all_gather(first, 'tensor', axis=1, tiled=True)]
    pallas_call x0 -> x1, Pallas kernels: none -> 98.8 us  [on_device(): pl.pallas_call(functools.partial(kernel, (n_dp, n_exp, nz, tok, feat, hid...]
    all_to_all x2 -> x0, blocking collectives: 86 us -> none  [the longest x1 44.2 us: send_out(): lax.all_to_all(second, 'expert', split_axis=0, concat_axis=0, tiled=True)]
    all_to_all x2 -> x0, starting transfers between devices: 57 us -> none  [the longest x1 28.8 us: send_back(): lax.all_to_all(first, 'expert', split_axis=0, concat_axis=0, tiled=True)]
    reduce_scatter x1 -> x0, waiting for transfers between devices: 34.2 us -> none  [on_device(): lax.psum_scatter(jnp.concatenate([first, second, third], axis=1).astype(j...]
    all_to_all x2 -> x0, waiting for transfers between devices: 18.9 us -> none  [the longest x1 18.9 us: send_back(): lax.all_to_all(second, 'expert', split_axis=0, concat_axis=0, tiled=True)]
    dot_general x14 -> x0, matrix products: 12.5 us -> none  [the longest x1 1.9 us: on_device(): gate_val = jnp.dot(expert_rows, w_gate, preferred_element_type=jnp.float32)]
  transfers between devices with their start and end apart: 5 -> 0, of which waited for: 4 -> 0; matrix products, arithmetic and copies ran while one was open for 1% -> 0% of each run, Pallas kernels for 0% -> 0%
where the time goes in v1:
time: 111 us
  Pallas kernels  98.8 us (89%)
  local copies, waits for them, and re-layouts  11.2 us (10%)
    pallas_call x1, Pallas kernels, on_device(): pl.pallas_call(functools.partial(kernel, (n_dp, n_exp, nz, tok, feat, hid...  98.8 us
    unnamed x18, local copies, waits for them, and re-layouts  11.2 us

profile of v1, /device:TPU:1, one launch (start us, length us, event | category | flops | bytes accessed | tf_op | source)
XLA Modules:
  0.0 110.6 jit_solution(9155807531366130264)
XLA Ops:
  0.6 0.8 copy.13.ids_ref
  1.4 0.8 copy.14.logit_ref
  2.2 0.0 copy-start
  2.2 1.4 %copy-done = bf16[1,3072,256]{2,1,0:T(8,128)(2,1)S(1)} copy-done((bf16[1,3072,256]{2,1,0:T(8,128)(2,1)S(1)}, bf16[1,3072,256]{2,1,0:T(8,128)(2,1)}, u32[]{:S(2)}) %copy-start) | copy-done | bytes 1572888
  3.6 0.0 copy-start.1
  3.6 1.4 %copy-done.1 = bf16[1,3072,256]{2,1,0:T(8,128)(2,1)S(1)} copy-done((bf16[1,3072,256]{2,1,0:T(8,128)(2,1)S(1)}, bf16[1,3072,256]{2,1,0:T(8,128)(2,1)}, u32[]{:S(2)}) %copy-start.1) | copy-done | bytes 1572888
  5.0 0.0 copy-start.2
  5.0 1.4 %copy-done.2 = bf16[1,3072,256]{2,1,0:T(8,128)(2,1)S(1)} copy-done((bf16[1,3072,256]{2,1,0:T(8,128)(2,1)S(1)}, bf16[1,3072,256]{2,1,0:T(8,128)(2,1)}, u32[]{:S(2)}) %copy-start.2) | copy-done | bytes 1572888
  6.4 0.0 copy-start.3
  6.4 0.7 copy-done.3
  7.1 0.0 copy-start.4
  7.1 0.7 copy-done.4
  7.8 98.8 %shard_map.118 = (bf16[32,96]{1,0:T(8,128)(2,1)S(1)}, bf16[32,96]{1,0:T(8,128)(2,1)S(1)}, f32[32,2]{1,0:T(8,128)S(1)}, bf16[768,256]{1,0:T(8,128)(2,1)S(1)}, bf1...) custom-call(bf16[32,96]{1,0:T(8,128)(2,1)S(1)} %copy-done.3, s32[32,2]{1,0:T(8,128)S(1)} %copy.13.ids_ref, ...), custom_call_target="tpu_custom_call" | custom-call | tf_op jit(solution)/shard_map/pallas_call | solution.py:507
  106.6 0.6 copy.15
  107.2 0.6 copy.21
  107.8 0.6 copy.22
  108.4 0.7 copy.23
  109.1 0.7 copy.24
  109.9 0.7 copy.25
Async XLA Ops:
  2.2 1.4 %copy-start = (bf16[1,3072,256]{2,1,0:T(8,128)(2,1)S(1)}, bf16[1,3072,256]{2,1,0:T(8,128)(2,1)}, u32[]{:S(2)}) copy-start(bf16[1,3072,256]{2,1,0:T(8,128)(2,1)} %param.10) | copy-start | bytes 4718596
  3.6 1.4 %copy-start.1 = (bf16[1,3072,256]{2,1,0:T(8,128)(2,1)S(1)}, bf16[1,3072,256]{2,1,0:T(8,128)(2,1)}, u32[]{:S(2)}) copy-start(bf16[1,3072,256]{2,1,0:T(8,128)(2,1)} %param.11) | copy-start | bytes 4718596
  5.0 1.4 %copy-start.2 = (bf16[1,3072,256]{2,1,0:T(8,128)(2,1)S(1)}, bf16[1,3072,256]{2,1,0:T(8,128)(2,1)}, u32[]{:S(2)}) copy-start(bf16[1,3072,256]{2,1,0:T(8,128)(2,1)} %param.12) | copy-start | bytes 4718596
  6.4 0.7 copy-start.3
  7.1 0.7 copy-start.4

commit v2 on v1

v2 whole, which is shorter than its diff:
```python
import functools

import jax
import jax.numpy as jnp
from jax import lax
from jax.experimental import pallas as pl
from jax.experimental.pallas import tpu as pltpu
from jax.sharding import PartitionSpec as P

MESH = pl.DeviceIdType.MESH
F32 = jnp.float32
BF16 = jnp.bfloat16
Y = 2


def dot(a, b):
    return jnp.dot(a, b, preferred_element_type=F32)


def dot_tn(a, b):
    return lax.dot_general(a, b, (((0,), (0,)), ((), ())), preferred_element_type=F32)


def dot_nt(a, b, precision=None):
    return lax.dot_general(
        a, b, (((1,), (1,)), ((), ())), precision=precision, preferred_element_type=F32
    )


def eye(n):
    rows = lax.broadcasted_iota(jnp.int32, (n, n), 0)
    cols = lax.broadcasted_iota(jnp.int32, (n, n), 1)
    return (rows == cols).astype(F32).astype(BF16)


def kernel(
    sizes,
    tok_hbm,
    ids_hbm,
    logit_hbm,
    wg_hbm,
    wu_hbm,
    wd_hbm,
    og_hbm,
    mixed_hbm,
    in_grad_hbm,
    logit_grad_hbm,
    gate_grad_hbm,
    up_grad_hbm,
    down_grad_hbm,
    tok_ref,
    ids_ref,
    logit_ref,
    og_ref,
    mixed_ref,
    in_grad_ref,
    logit_grad_ref,
    grads_ref,
    wg,
    wu,
    wd,
    stage,
    out0,
    in0,
    xg,
    acc,
    hid,
    xq,
    hq,
    terms,
    pair_out,
    pair_in,
    z_out,
    z_in,
    sw_q,
    sw_r,
    sw_y,
    sw_all,
    out4,
    in4,
    load_sem,
    store_sem,
    s0_sem,
    r0_sem,
    sy_sem,
    ry_sem,
    sg_sem,
    rg_sem,
    xq_s,
    xq_r,
    hq_s,
    hq_r,
    sp_sem,
    rp_sem,
    sz_sem,
    rz_sem,
    swq_s,
    swq_r,
    swr_s,
    swr_r,
    swy_s,
    swy_r,
    swx_s,
    swx_r,
    s4_sem,
    r4_sem,
):
    n_dp, n_exp, nz, tok, feat, hidw, pad = sizes
    slot = tok // 2
    rows = n_exp * slot
    half_ring = nz // 2
    groups = nz // 4
    planes = nz // n_dp
    d = lax.axis_index("dp")
    e = lax.axis_index("expert")
    t_me = lax.axis_index("tensor")
    z, y = t_me // Y, t_me % Y
    y_other = 1 - y

    def at_z(off):
        return lax.rem(z + (off + nz), nz)

    def device(off):
        return {"tensor": at_z(off) * Y + y}

    pair = {"tensor": z * Y + y_other}

    z_peers = [1, -1, 2] + ([-2] if nz > 4 else [])
    z_peers += [4 * k for k in range(1, groups) if nz > 4]
    peers = [device(off) for off in z_peers] + [pair]
    peers += [{"expert": lax.rem(e + o, n_exp)} for o in range(1, n_exp)]
    peers += [{"dp": lax.rem(d + o, n_dp)} for o in range(1, n_dp)]
    barrier = pltpu.get_barrier_semaphore()
    for peer in peers:
        pl.semaphore_signal(barrier, inc=1, device_id=peer, device_id_type=MESH)

    loads = [
        pltpu.make_async_copy(src, dst, load_sem.at[i])
        for i, (src, dst) in enumerate(
            (
                (ids_hbm, ids_ref),
                (logit_hbm, logit_ref),
                (tok_hbm, tok_ref),
                (og_hbm, og_ref),
                (wg_hbm, wg),
                (wu_hbm, wu),
                (wd_hbm, wd),
            )
        )
    ]
    for load in loads:
        load.start()

    def remote(src, dst, send, recv, peer):
        return pltpu.make_async_remote_copy(
            src_ref=src,
            dst_ref=dst,
            send_sem=send,
            recv_sem=recv,
            device_id=peer,
            device_id_type=MESH,
        )

    stage[...] = jnp.zeros_like(stage)
    out4[...] = jnp.zeros_like(out4)
    acc[...] = jnp.zeros_like(acc)
    later = lax.broadcasted_iota(jnp.int32, (tok, tok), 0)
    earlier = lax.broadcasted_iota(jnp.int32, (tok, tok), 1)
    before = (earlier < later).astype(F32).astype(BF16)
    lanes = lax.broadcasted_iota(jnp.int32, (tok, 128), 1)
    row_lane = lax.broadcasted_iota(jnp.int32, (tok, rows), 1)

    def column(line):
        return jnp.sum(jnp.where(later == earlier, line, 0), axis=1, keepdims=True)

    for load in loads[:2]:
        load.wait()
    ids = ids_ref[...].astype(F32)
    logits = logit_ref[...]
    id_k = [column(ids[k : k + 1, :]).astype(jnp.int32) for k in range(2)]
    hot = [(lanes == i).astype(F32) for i in id_k]
    count = dot(before, (hot[0] + hot[1]).astype(BF16))
    place = [jnp.sum(h * count, axis=1, keepdims=True).astype(jnp.int32) for h in hot]
    select = [
        (row_lane == i * slot + p).astype(F32).astype(BF16) for i, p in zip(id_k, place)
    ]
    diff = column(logits[0:1, :] - logits[1:2, :])
    share = (jax.nn.sigmoid(diff), jax.nn.sigmoid(-diff))

    for load in loads[2:4]:
        load.wait()
    tokens = tok_ref[...]
    grads = og_ref[...].astype(F32)
    for k in range(2):
        stage[k * tok : (k + 1) * tok, 0:feat] = tokens
        stage[k * tok : (k + 1) * tok, pad : pad + feat] = (share[k] * grads).astype(BF16)
    placed = dot_tn(jnp.concatenate(select, axis=0), stage[...]).astype(BF16)
    out0[...] = placed.reshape(n_exp, slot, 2 * pad)

    pl.semaphore_wait(barrier, len(peers))

    def swap(src, dst, send, recv, o):
        to = lax.rem(e + o, n_exp)
        return remote(src.at[to], dst.at[e], send.at[o - 1], recv.at[o - 1], {"expert": to})

    for o in range(1, n_exp):
        swap(out0, in0, s0_sem, r0_sem, o).start()
    in0[pl.ds(e, 1)] = out0[pl.ds(e, 1)]
    for o in range(1, n_exp):
        swap(out0, in0, s0_sem, r0_sem, o).wait_recv()

    unit = eye(pad)
    for a in range(2):
        arrived = in0[:, :, a * pad : (a + 1) * pad].reshape(rows, pad)
        turned = dot_nt(unit, arrived)
        xg[pl.ds(z, 1), pl.ds(y, 1), a] = turned[0:feat].astype(BF16)[None, None]

    def step(kind, i):
        off, to, half = {
            "chain_up": (-2 * i, 2, y),
            "chain_down": (2 * i, -2, y),
            "near_up": (-2 * i, 1, y),
            "near_down": (2 * i, -1, y),
            "both_down": (2 * i, -1, y_other),
        }[kind]
        n = ("chain_up", "chain_down", "near_up", "near_down", "both_down").index(kind)
        ref = xg.at[at_z(off), half]
        return remote(ref, ref, sg_sem.at[n, i], rg_sem.at[n, i], device(to))

    def across(off):
        ref = xg.at[at_z(off), y]
        return remote(ref, ref, sy_sem.at[off % nz], ry_sem.at[off % nz], pair)

    relayed = [2 * i + 1 for i in range(groups - 1)]

    def quarter(o, p):
        peer = lax.rem(d + o, n_dp)
        return remote(
            xg.at[peer * planes + p],
            xq.at[o - 1, p],
            xq_s.at[o - 1, p],
            xq_r.at[o - 1, p],
            {"dp": peer},
        )

    def complete(off):
        if off in relayed:
            step("both_down", (off - 1) // 2).wait_recv()
        else:
            across(off).wait_recv()
            if off >= 0 and off % 2 == 0 and off // 2 < groups - 1:
                step("both_down", off // 2).start()

    def accumulate(block):
        both = xg[pl.ds(block, 1)]
        xt = both[0, :, 0].reshape(Y * feat, rows)
        gt = both[0, :, 1].reshape(Y * feat, rows)
        acc[0] += dot_tn(xt, wg[pl.ds(block, 1)][0])
        acc[1] += dot_tn(xt, wu[pl.ds(block, 1)][0])
        acc[2] += dot_tn(gt, wd[pl.ds(block, 1)][0])

    def forward(block):
        peer, p = block // planes, lax.rem(block, planes)
        o = lax.rem(peer - d + n_dp, n_dp)

        @pl.when(o > 0)
        def _():
            remote(
                xg.at[block],
                xq.at[o - 1, p],
                xq_s.at[o - 1, p],
                xq_r.at[o - 1, p],
                {"dp": peer},
            ).start()

    def plane_group(i):
        if i == 0:
            return [0]
        offs = [-2 * i, 2 * i, -(2 * i - 1), 2 * i - 1]
        if i == groups:
            offs.remove(2 * i)
        return offs

    def use(i):
        offs = plane_group(i)
        for off in offs:
            complete(off)
        if i == 0:
            accumulate(z)
            forward(z)
            return

        @pl.loop(0, len(offs))
        def _(j):
            at = j + (j > 0).astype(jnp.int32) if i == groups else j
            off = (2 * lax.rem(at, 2) - 1) * (2 * i - at // 2)
            block = lax.rem(z + off + nz, nz)
            accumulate(block)
            forward(block)

    step("chain_up", 0).start()
    if groups > 1:
        step("chain_down", 0).start()
    across(0).start()
    step("near_up", 0).start()
    step("near_down", 0).start()
    for load in loads[4:]:
        load.wait()
    for i in range(1, groups + 1):
        step("chain_up", i - 1).wait_recv()
        if i < groups:
            step("chain_up", i).start()
            step("near_up", i).start()
            step("chain_down", i - 1).wait_recv()
            if i < groups - 1:
                step("chain_down", i).start()
            step("near_down", i).start()
        for off in plane_group(i):
            if off == -(2 * i - 1):
                step("near_up", i - 1).wait_recv()
            if off == 2 * i - 1:
                step("near_down", i - 1).wait_recv()
            if off not in relayed:
                across(off).start()
        use(i - 1)
    use(groups)

    def factors(o):
        return remote(
            hid, hq.at[o - 1], hq_s.at[o - 1], hq_r.at[o - 1], {"dp": lax.rem(d + o, n_dp)}
        )

    gate, lift, hid_grad = acc[0], acc[1], acc[2]
    sigma = jax.nn.sigmoid(gate)
    active = gate * sigma
    hidden = active * lift
    hid[:, 0:hidw] = hidden.astype(BF16)
    hid[:, hidw : 2 * hidw] = (
        hid_grad * lift * sigma * (1.0 + gate * (1.0 - sigma))
    ).astype(BF16)
    hid[:, 2 * hidw : 3 * hidw] = (hid_grad * active).astype(BF16)

    def own(block, a):
        if a == 0:
            return dot_nt(wd[pl.ds(block, 1)][0], hid[:, 0:hidw])
        return dot_nt(wg[pl.ds(block, 1)][0], hid[:, hidw : 2 * hidw]) + dot_nt(
            wu[pl.ds(block, 1)][0], hid[:, 2 * hidw : 3 * hidw]
        )

    UP, NEAR_DOWN, NEAR_UP, DOWN = range(4)
    sends_to = (2, -1, 1, -2)

    def target(g, j):
        return (
            half_ring - 2 * g,
            -(half_ring - 1) + 2 * g,
            half_ring - 1 - 2 * g,
            -(half_ring - 2) + 2 * g,
        )[j]

    def to_pair(n):
        return remote(pair_out.at[n], pair_in.at[n], sp_sem.at[n], rp_sem.at[n], pair)

    def along(j, g):
        return remote(
            z_out.at[j, g], z_in.at[j, g], sz_sem.at[j, g], rz_sem.at[j, g], device(sends_to[j])
        )

    def prepare(g):
        for j in (NEAR_DOWN, NEAR_UP, UP, DOWN):
            n = 4 * g + j
            block = at_z(target(g, j))
            for a in range(2):
                terms[n, a] = own(block, a).reshape(Y, feat, rows)
                pair_out[n, a] = terms[n, a, pl.ds(y_other, 1)][0].astype(BF16)
            to_pair(n).start()

    def settle(g, j, extra, send):
        n = 4 * g + j
        to_pair(n).wait_recv()
        for kind, i in extra:
            along(kind, i).wait_recv()
        totals = []
        for a in range(2):
            total = terms[n, a, pl.ds(y, 1)][0] + pair_in[n, a].astype(F32)
            for kind, i in extra:
                total = total + z_in[kind, i, a].astype(F32)
            if send:
                z_out[j, g, a] = total.astype(BF16)
            totals.append(total)
        if send:
            along(j, g).start()
        return totals

    prepare(0)
    for o in range(1, n_dp):
        factors(o).start()

    quad, place4 = z // 4, lax.rem(z, 4)

    def sw_quads(k):
        return remote(
            sw_q.at[quad], sw_q.at[quad], swq_s.at[k - 1], swq_r.at[k - 1], device(4 * k)
        )

    def sw_near(k):
        return remote(
            sw_r.at[place4], sw_r.at[place4], swr_s.at[k], swr_r.at[k], device((1, -1, -2)[k])
        )

    def sw_pair():
        return remote(sw_y.at[y], sw_y.at[y], swy_s, swy_r, pair)

    def sw_swap(o):
        return remote(
            sw_all.at[e],
            sw_all.at[e],
            swx_s.at[o - 1],
            swx_r.at[o - 1],
            {"expert": lax.rem(e + o, n_exp)},
        )

    line = dot_nt(jnp.ones((8, hidw), F32), hidden * hid_grad, lax.Precision.HIGHEST)
    sw_q[pl.ds(quad, 1)] = line[None]
    for k in range(1, groups):
        sw_quads(k).start()

    def sw_first():
        for k in range(1, groups):
            sw_quads(k).wait_recv()
        total = sw_q[0]
        for i in range(1, groups):
            total = total + sw_q[i]
        sw_r[pl.ds(place4, 1)] = total[None]
        for k in range(3):
            sw_near(k).start()

    def sw_second():
        for k in range(3):
            sw_near(k).wait_recv()
        sw_y[pl.ds(y, 1)] = (((sw_r[0] + sw_r[1]) + sw_r[2]) + sw_r[3])[None]
        sw_pair().start()

    def sw_third():
        sw_pair().wait_recv()
        sw_all[pl.ds(e, 1)] = (sw_y[0] + sw_y[1])[None]
        for o in range(1, n_exp):
            sw_swap(o).start()

    sw_stages = [sw_first, sw_second, sw_third]
    for g in range(groups):
        if g + 1 < groups:
            prepare(g + 1)
        settle(g, NEAR_DOWN, [], True)
        settle(g, NEAR_UP, [], True)
        settle(g, UP, [(UP, g - 1), (NEAR_UP, g - 1)] if g > 0 else [], True)
        extra = [(NEAR_DOWN, g)] + ([(DOWN, g - 1)] if g > 0 else [])
        if g < groups - 1:
            settle(g, DOWN, extra, True)
            if g > 0:
                sw_stages.pop(0)()
        else:
            totals = settle(g, DOWN, extra + [(UP, g), (NEAR_UP, g)], False)

    back = eye(rows)
    for a in range(2):
        turned = dot_nt(back, totals[a].astype(BF16)).astype(BF16)
        out4[:, :, a * pad : a * pad + feat] = turned.reshape(n_exp, slot, feat)
    for o in range(1, n_exp):
        swap(out4, in4, s4_sem, r4_sem, o).start()
    in4[pl.ds(e, 1)] = out4[pl.ds(e, 1)]
    for sw_stage in sw_stages:
        sw_stage()

    for o in range(1, n_dp):
        for p in range(planes):
            quarter(o, p).wait_recv()
        factors(o).wait_recv()

    @pl.loop(0, planes)
    def _(p):
        both = [xg[pl.ds(d * planes + p, 1)][0]] + [
            xq[o, pl.ds(p, 1)][0] for o in range(n_dp - 1)
        ]
        parts = [hid] + [hq.at[o] for o in range(n_dp - 1)]
        here = pl.ds(pl.multiple_of(p * Y * feat, Y * feat), Y * feat)
        for n, a, i in ((0, 0, 1), (1, 0, 2), (2, 1, 0)):
            total = None
            for b, h in zip(both, parts):
                term = dot(b[:, a].reshape(Y * feat, rows), h[:, i * hidw : (i + 1) * hidw])
                total = term if total is None else total + term
            grads_ref[n, here, :] = total.astype(BF16)

    stores = [
        pltpu.make_async_copy(src, dst, store_sem.at[i])
        for i, (src, dst) in enumerate(
            (
                (grads_ref.at[0], gate_grad_hbm),
                (grads_ref.at[1], up_grad_hbm),
                (grads_ref.at[2], down_grad_hbm),
                (mixed_ref, mixed_hbm),
                (in_grad_ref, in_grad_hbm),
                (logit_grad_ref, logit_grad_hbm),
            )
        )
    ]
    for store in stores[:3]:
        store.start()

    for o in range(1, n_exp):
        swap(out4, in4, s4_sem, r4_sem, o).wait_recv()
    came = in4[...].reshape(rows, 2 * pad)
    picked = [dot(s, came) for s in select]
    mixed_ref[...] = (
        share[0] * picked[0][:, 0:feat] + share[1] * picked[1][:, 0:feat]
    ).astype(BF16)
    in_grad_ref[...] = (
        picked[0][:, pad : pad + feat] + picked[1][:, pad : pad + feat]
    ).astype(BF16)
    for store in stores[3:5]:
        store.start()
    for o in range(1, n_exp):
        sw_swap(o).wait_recv()
    sw = []
    for k in range(2):
        line = jnp.zeros((tok, rows), F32)
        for i in range(n_exp):
            line = line + hot[k][:, i : i + 1] * jnp.concatenate([sw_all[i]] * (tok // 8), axis=0)
        here = row_lane == e * slot + place[k]
        sw.append(jnp.sum(jnp.where(here, line, 0.0), axis=1, keepdims=True))
    first = jnp.sum(
        jnp.where(later == earlier, share[1] * sw[0] - share[0] * sw[1], 0.0),
        axis=0,
        keepdims=True,
    )
    which = lax.broadcasted_iota(jnp.int32, (2, tok), 0)
    logit_grad_ref[...] = jnp.where(which == 0, first, -first)
    stores[5].start()

    for o in range(1, n_exp):
        swap(out0, in0, s0_sem, r0_sem, o).wait_send()
        swap(out4, in4, s4_sem, r4_sem, o).wait_send()
        sw_swap(o).wait_send()
    for i in range(groups):
        step("chain_up", i).wait_send()
        step("near_up", i).wait_send()
        step("near_down", i).wait_send()
        if i < groups - 1:
            step("chain_down", i).wait_send()
            step("both_down", i).wait_send()
        for j in (NEAR_DOWN, NEAR_UP, UP, DOWN):
            to_pair(4 * i + j).wait_send()
            if j != DOWN or i < groups - 1:
                along(j, i).wait_send()
    for off in range(nz):
        if off not in relayed:
            across(off).wait_send()
    for o in range(1, n_dp):
        for p in range(planes):
            quarter(o, p).wait_send()
        factors(o).wait_send()
    for k in range(1, groups):
        sw_quads(k).wait_send()
    for k in range(3):
        sw_near(k).wait_send()
    sw_pair().wait_send()
    for store in stores:
        store.wait()


def hand_over(*refs):
    count = (len(refs) - 2) // 3
    sources, results, held = refs[:count], refs[count : 2 * count], refs[2 * count : 3 * count]
    in_sem, out_sem = refs[-2:]
    ins = [pltpu.make_async_copy(sources[i], held[i], in_sem.at[i]) for i in range(count)]
    outs = [pltpu.make_async_copy(held[i], results[i], out_sem.at[i]) for i in range(count)]
    for copy in ins:
        copy.start()
    for before, after in zip(ins, outs):
        before.wait()
        after.start()
    for copy in outs:
        copy.wait()


def solution(mesh):
    n_dp, n_exp, n_t = mesh.shape["dp"], mesh.shape["expert"], mesh.shape["tensor"]
    nz = n_t // Y

    def on_device(tokens, expert_ids, gate_logits, gate_weight, up_weight, down_weight, out_grad):
        tok, feat = tokens.shape
        hidw = gate_weight.shape[2]
        slot = tok // 2
        rows = n_exp * slot
        groups = nz // 4
        planes = nz // n_dp
        pad = -(-feat // 128) * 128
        width = feat * n_t // n_dp
        hbm = pl.BlockSpec(memory_space=pl.ANY)
        dma = pltpu.SemaphoreType.DMA
        weights = [w.reshape(nz, Y * feat, hidw) for w in (gate_weight, up_weight, down_weight)]
        grad = jax.ShapeDtypeStruct((width, hidw), BF16)
        shapes = (
            jax.ShapeDtypeStruct((tok, feat), BF16),
            jax.ShapeDtypeStruct((tok, feat), BF16),
            jax.ShapeDtypeStruct((2, tok), F32),
            grad,
            grad,
            grad,
        )
        block = (2, feat, rows)
        outs = pl.pallas_call(
            functools.partial(kernel, (n_dp, n_exp, nz, tok, feat, hidw, pad)),
            out_shape=shapes,
            in_specs=[hbm] * 7,
            out_specs=[hbm] * 6,
            scratch_shapes=[
                pltpu.VMEM((tok, feat), BF16),
                pltpu.VMEM((2, tok), jnp.int32),
                pltpu.VMEM((2, tok), F32),
                pltpu.VMEM((tok, feat), BF16),
                pltpu.VMEM((tok, feat), BF16),
                pltpu.VMEM((tok, feat), BF16),
                pltpu.VMEM((2, tok), F32),
                pltpu.VMEM((3, width, hidw), BF16),
                pltpu.VMEM((nz, Y * feat, hidw), BF16),
                pltpu.VMEM((nz, Y * feat, hidw), BF16),
                pltpu.VMEM((nz, Y * feat, hidw), BF16),
                pltpu.VMEM((2 * tok, 2 * pad), BF16),
                pltpu.VMEM((n_exp, slot, 2 * pad), BF16),
                pltpu.VMEM((n_exp, slot, 2 * pad), BF16),
                pltpu.VMEM((nz, Y) + block, BF16),
                pltpu.VMEM((3, rows, hidw), F32),
                pltpu.VMEM((rows, 3 * hidw), BF16),
                pltpu.VMEM((n_dp - 1, planes, Y) + block, BF16),
                pltpu.VMEM((n_dp - 1, rows, 3 * hidw), BF16),
                pltpu.VMEM((nz, 2, Y, feat, rows), F32),
                pltpu.VMEM((nz,) + block, BF16),
                pltpu.VMEM((nz,) + block, BF16),
                pltpu.VMEM((4, groups) + block, BF16),
                pltpu.VMEM((4, groups) + block, BF16),
                pltpu.VMEM((groups, 8, rows), F32),
                pltpu.VMEM((4, 8, rows), F32),
                pltpu.VMEM((Y, 8, rows), F32),
                pltpu.VMEM((n_exp, 8, rows), F32),
                pltpu.VMEM((n_exp, slot, 2 * pad), BF16),
                pltpu.VMEM((n_exp, slot, 2 * pad), BF16),
                dma((7,)),
                dma((6,)),
                dma((n_exp - 1,)),
                dma((n_exp - 1,)),
                dma((nz,)),
                dma((nz,)),
                dma((5, groups)),
                dma((5, groups)),
                dma((n_dp - 1, planes)),
                dma((n_dp - 1, planes)),
                dma((n_dp - 1,)),
                dma((n_dp - 1,)),
                dma((nz,)),
                dma((nz,)),
                dma((4, groups)),
                dma((4, groups)),
                dma((max(groups - 1, 1),)),
                dma((max(groups - 1, 1),)),
                dma((3,)),
                dma((3,)),
                dma,
                dma,
                dma((n_exp - 1,)),
                dma((n_exp - 1,)),
                dma((n_exp - 1,)),
                dma((n_exp - 1,)),
            ],
            compiler_params=pltpu.CompilerParams(
                collective_id=0, has_side_effects=True, vmem_limit_bytes=60 * 1024 * 1024
            ),
        )(tokens, expert_ids.T, gate_logits.T, *weights, out_grad)
        mixed, in_grad, logit_grad, gate_grad, up_grad, down_grad = pl.pallas_call(
            hand_over,
            out_shape=shapes,
            in_specs=[hbm] * 6,
            out_specs=[hbm] * 6,
            scratch_shapes=[pltpu.VMEM(out.shape, out.dtype) for out in shapes]
            + [dma((6,)), dma((6,))],
            compiler_params=pltpu.CompilerParams(vmem_limit_bytes=60 * 1024 * 1024),
        )(*outs)
        return mixed, in_grad, logit_grad.T, gate_grad[None], up_grad[None], down_grad[None]

    return jax.shard_map(
        on_device,
        mesh=mesh,
        in_specs=(
            P(("dp", "expert"), "tensor"),
            P(("dp", "expert"), None),
            P(("dp", "expert"), None),
            P("expert", None, "tensor"),
            P("expert", None, "tensor"),
            P("expert", None, "tensor"),
            P(("dp", "expert"), "tensor"),
        ),
        out_specs=(
            P(("dp", "expert"), "tensor"),
            P(("dp", "expert"), "tensor"),
            P(("dp", "expert"), None),
            P("expert", "dp", "tensor"),
            P("expert", "dp", "tensor"),
            P("expert", "dp", "tensor"),
        ),
        check_vma=False,
    )
```

time: 111 us -> 86.1 us (0.78)
  Pallas kernels: 98.8 us -> 85.3 us
  local copies, waits for them, and re-layouts: 11.2 us -> 0 us
    pallas_call x1, Pallas kernels: 98.8 us -> 83.1 us  [on_device(): pl.pallas_call(functools.partial(kernel, (n_dp, n_exp, nz, tok, feat, hid...]
    unnamed x18 -> x0, local copies, waits for them, and re-layouts: 11.2 us -> none
    pallas_call x0 -> x1, Pallas kernels: none -> 2.14 us  [on_device(): pl.pallas_call(hand_over, out_shape=shapes, in_specs=[hbm] * 6, out_specs...]
where the time goes in v2:
time: 86.1 us; the launch traced here: 85.9 us
  Pallas kernels  85.3 us (99%)
    pallas_call x1, Pallas kernels, on_device(): pl.pallas_call(functools.partial(kernel, (n_dp, n_exp, nz, tok, feat, hid...  83.1 us
    pallas_call x1, Pallas kernels, on_device(): pl.pallas_call(hand_over, out_shape=shapes, in_specs=[hbm] * 6, out_specs...  2.14 us

profile of v2, /device:TPU:1, one launch (start us, length us, event | category | flops | bytes accessed | tf_op | source)
XLA Modules:
  0.0 85.9 jit_solution(4620184796713032591)
XLA Ops:
  0.6 83.1 %shard_map.118 = (bf16[32,96]{1,0:T(8,128)(2,1)}, bf16[32,96]{1,0:T(8,128)(2,1)}, f32[2,32]{1,0:T(2,128)}, bf16[768,256]{1,0:T(8,128)(2,1)}, bf16[768,256]{1,0:T(8,128)(2,1)}, /*index=5*/bf16[768,256]{1,0:T(8,128)(2,1)}) custom-call(bf16[32,96]{1,0:T(8,128)(2,1)} %tok_hbm.1, s32[2,32]{1,0:T(2,128)} %bitcast.12, f32[2,32]{1,0:T(2,128)} %bitcast.13, ...), custom_call_target="tpu_custom_call" | custom-call | tf_op jit(solution)/shard_map/pallas_call | solution.py:612
  83.8 2.1 %shard_map.119 = (bf16[32,96]{1,0:T(8,128)(2,1)}, bf16[32,96]{1,0:T(8,128)(2,1)}, f32[2,32]{1,0:T(2,128)}, bf16[768,256]{1,0:T(8,128)(2,1)}, bf16[768,256]{1,0:T(8,128)(2,1)}, /*index=5*/bf16[768,256]{1,0:T(8,128)(2,1)}) custom-call(bf16[32,96]{1,0:T(8,128)(2,1)} %get-tuple-element.18.refs_0_, bf16[32,96]{1,0:T(8,128)(2,1)} %get-tuple-element.19.refs_1_, ...), custom_call_target="tpu_custom_call" | custom-call | tf_op jit(solution)/shard_map/pallas_call | solution.py:679

commit v3 on v2

--- a/solution.py
+++ b/solution.py
@@ -31,6 +31,23 @@
     rows = lax.broadcasted_iota(jnp.int32, (n, n), 0)
     cols = lax.broadcasted_iota(jnp.int32, (n, n), 1)
     return (rows == cols).astype(F32).astype(BF16)
+
+
+def tree(nz):
+    groups = nz // 4
+    parent, levels, doubled = {}, [[0]], []
+    for i in range(groups):
+        up, down = [2 * i + 2, 2 * i + 1], [-2 * i - 1]
+        if i < groups - 1:
+            down.insert(0, -2 * i - 2)
+        if i > 0 and i >= groups - 2:
+            doubled.append(-2 * i - 1)
+        if i > 0 and i == groups - 1:
+            doubled.append(2 * i + 1)
+        parent.update({k: 2 * i for k in up})
+        parent.update({k: -2 * i for k in down})
+        levels.append([k for pair in zip(up, down) for k in pair] + up[len(down) :])
+    return parent, levels, tuple(doubled)
 
 
 def kernel(
@@ -72,8 +89,9 @@
     pair_in,
     z_out,
     z_in,
-    sw_q,
-    sw_r,
+    both_out,
+    both_in,
+    sw_z,
     sw_y,
     sw_all,
     out4,
@@ -86,6 +104,8 @@
     ry_sem,
     sg_sem,
     rg_sem,
+    sb_sem,
+    rb_sem,
     xq_s,
     xq_r,
     hq_s,
@@ -94,10 +114,10 @@
     rp_sem,
     sz_sem,
     rz_sem,
-    swq_s,
-    swq_r,
-    swr_s,
-    swr_r,
+    so_sem,
+    ro_sem,
+    swz_s,
+    swz_r,
     swy_s,
     swy_r,
     swx_s,
@@ -108,9 +128,13 @@
     n_dp, n_exp, nz, tok, feat, hidw, pad = sizes
     slot = tok // 2
     rows = n_exp * slot
-    half_ring = nz // 2
-    groups = nz // 4
     planes = nz // n_dp
+    parent, levels, doubled = tree(nz)
+    others = [k for level in levels[1:] for k in level]
+    children = {
+        k: sorted((c for c in others if parent[c] == k), key=lambda c: -abs(c - k))
+        for k in [0] + others
+    }
     d = lax.axis_index("dp")
     e = lax.axis_index("expert")
     t_me = lax.axis_index("tensor")
@@ -125,8 +149,8 @@
 
     pair = {"tensor": z * Y + y_other}
 
-    z_peers = [1, -1, 2] + ([-2] if nz > 4 else [])
-    z_peers += [4 * k for k in range(1, groups) if nz > 4]
+    hops = {k - parent[k] for k in others}
+    z_peers = sorted({h % nz for h in hops} | {-h % nz for h in hops})
     peers = [device(off) for off in z_peers] + [pair]
     peers += [{"expert": lax.rem(e + o, n_exp)} for o in range(1, n_exp)]
     peers += [{"dp": lax.rem(d + o, n_dp)} for o in range(1, n_dp)]
@@ -201,7 +225,7 @@
 
     def swap(src, dst, send, recv, o):
         to = lax.rem(e + o, n_exp)
-        return remote(src.at[to], dst.at[e], send.at[o - 1], recv.at[o - 1], {"expert": to})
+        return remote(src.at[to], dst.at[e], send, recv.at[o - 1], {"expert": to})
 
     for o in range(1, n_exp):
         swap(out0, in0, s0_sem, r0_sem, o).start()
@@ -215,41 +239,46 @@
         turned = dot_nt(unit, arrived)
         xg[pl.ds(z, 1), pl.ds(y, 1), a] = turned[0:feat].astype(BF16)[None, None]
 
-    def step(kind, i):
-        off, to, half = {
-            "chain_up": (-2 * i, 2, y),
-            "chain_down": (2 * i, -2, y),
-            "near_up": (-2 * i, 1, y),
-            "near_down": (2 * i, -1, y),
-            "both_down": (2 * i, -1, y_other),
-        }[kind]
-        n = ("chain_up", "chain_down", "near_up", "near_down", "both_down").index(kind)
-        ref = xg.at[at_z(off), half]
-        return remote(ref, ref, sg_sem.at[n, i], rg_sem.at[n, i], device(to))
-
-    def across(off):
-        ref = xg.at[at_z(off), y]
-        return remote(ref, ref, sy_sem.at[off % nz], ry_sem.at[off % nz], pair)
-
-    relayed = [2 * i + 1 for i in range(groups - 1)]
+    def deliver(c):
+        ref = xg.at[at_z(-parent[c]), y]
+        return remote(ref, ref, sg_sem, rg_sem.at[c % nz], device(c - parent[c]))
+
+    def deliver_other(c):
+        ref = xg.at[at_z(-parent[c]), y_other]
+        n = doubled.index(c)
+        return remote(ref, ref, sb_sem, rb_sem.at[n], device(c - parent[c]))
+
+    def arrive(c):
+        ref = xg.at[at_z(-c), y]
+        remote(ref, ref, sg_sem, rg_sem.at[c % nz], device(c - parent[c])).wait_recv()
+
+    def arrive_other(c):
+        ref = xg.at[at_z(-c), y_other]
+        n = doubled.index(c)
+        remote(ref, ref, sb_sem, rb_sem.at[n], device(c - parent[c])).wait_recv()
+
+    def across(k):
+        ref = xg.at[at_z(-k), y]
+        return remote(ref, ref, sy_sem, ry_sem.at[k % nz], pair)
 
     def quarter(o, p):
         peer = lax.rem(d + o, n_dp)
         return remote(
             xg.at[peer * planes + p],
             xq.at[o - 1, p],
-            xq_s.at[o - 1, p],
+            xq_s,
             xq_r.at[o - 1, p],
             {"dp": peer},
         )
 
-    def complete(off):
-        if off in relayed:
-            step("both_down", (off - 1) // 2).wait_recv()
+    def complete(k):
+        if k in doubled:
+            arrive_other(k)
         else:
-            across(off).wait_recv()
-            if off >= 0 and off % 2 == 0 and off // 2 < groups - 1:
-                step("both_down", off // 2).start()
+            across(k).wait_recv()
+            for c in children[k]:
+                if c in doubled:
+                    deliver_other(c).start()
 
     def accumulate(block):
         both = xg[pl.ds(block, 1)]
@@ -268,66 +297,45 @@
             remote(
                 xg.at[block],
                 xq.at[o - 1, p],
-                xq_s.at[o - 1, p],
+                xq_s,
                 xq_r.at[o - 1, p],
                 {"dp": peer},
             ).start()
 
-    def plane_group(i):
-        if i == 0:
-            return [0]
-        offs = [-2 * i, 2 * i, -(2 * i - 1), 2 * i - 1]
-        if i == groups:
-            offs.remove(2 * i)
-        return offs
-
-    def use(i):
-        offs = plane_group(i)
-        for off in offs:
-            complete(off)
-        if i == 0:
-            accumulate(z)
-            forward(z)
-            return
-
-        @pl.loop(0, len(offs))
-        def _(j):
-            at = j + (j > 0).astype(jnp.int32) if i == groups else j
-            off = (2 * lax.rem(at, 2) - 1) * (2 * i - at // 2)
-            block = lax.rem(z + off + nz, nz)
-            accumulate(block)
-            forward(block)
-
-    step("chain_up", 0).start()
-    if groups > 1:
-        step("chain_down", 0).start()
-    across(0).start()
-    step("near_up", 0).start()
-    step("near_down", 0).start()
-    for load in loads[4:]:
-        load.wait()
-    for i in range(1, groups + 1):
-        step("chain_up", i - 1).wait_recv()
-        if i < groups:
-            step("chain_up", i).start()
-            step("near_up", i).start()
-            step("chain_down", i - 1).wait_recv()
-            if i < groups - 1:
-                step("chain_down", i).start()
-            step("near_down", i).start()
-        for off in plane_group(i):
-            if off == -(2 * i - 1):
-                step("near_up", i - 1).wait_recv()
-            if off == 2 * i - 1:
-                step("near_down", i - 1).wait_recv()
-            if off not in relayed:
-                across(off).start()
-        use(i - 1)
-    use(groups)
+    early = sorted({parent[c] for c in doubled})
+
+    def use(level):
+        for k in levels[level]:
+            if k not in early:
+                complete(k)
+            accumulate(at_z(-k))
+            forward(at_z(-k))
+
+    for level, offsets in enumerate(levels):
+        for k in offsets:
+            if level > 0:
+                arrive(k)
+            far = [c for c in children[k] if abs(c - k) > 1]
+            for c in far:
+                deliver(c).start()
+            if k not in doubled:
+                across(k).start()
+            for c in children[k]:
+                if c not in far:
+                    deliver(c).start()
+        if level == 0:
+            for load in loads[4:]:
+                load.wait()
+        else:
+            use(level - 1)
+        for k in offsets:
+            if k in early:
+                complete(k)
+    use(len(levels) - 1)
 
     def factors(o):
         return remote(
-            hid, hq.at[o - 1], hq_s.at[o - 1], hq_r.at[o - 1], {"dp": lax.rem(d + o, n_dp)}
+            hid, hq.at[o - 1], hq_s, hq_r.at[o - 1], {"dp": lax.rem(d + o, n_dp)}
         )
 
     gate, lift, hid_grad = acc[0], acc[1], acc[2]
@@ -347,66 +355,84 @@
             wu[pl.ds(block, 1)][0], hid[:, 2 * hidw : 3 * hidw]
         )
 
-    UP, NEAR_DOWN, NEAR_UP, DOWN = range(4)
-    sends_to = (2, -1, 1, -2)
-
-    def target(g, j):
-        return (
-            half_ring - 2 * g,
-            -(half_ring - 1) + 2 * g,
-            half_ring - 1 - 2 * g,
-            -(half_ring - 2) + 2 * g,
-        )[j]
-
-    def to_pair(n):
-        return remote(pair_out.at[n], pair_in.at[n], sp_sem.at[n], rp_sem.at[n], pair)
-
-    def along(j, g):
+    def to_pair(k):
+        n = k % nz
+        return remote(pair_out.at[n], pair_in.at[n], sp_sem, rp_sem.at[n], pair)
+
+    def along(k):
+        n = k % nz
         return remote(
-            z_out.at[j, g], z_in.at[j, g], sz_sem.at[j, g], rz_sem.at[j, g], device(sends_to[j])
-        )
-
-    def prepare(g):
-        for j in (NEAR_DOWN, NEAR_UP, UP, DOWN):
-            n = 4 * g + j
-            block = at_z(target(g, j))
-            for a in range(2):
-                terms[n, a] = own(block, a).reshape(Y, feat, rows)
-                pair_out[n, a] = terms[n, a, pl.ds(y_other, 1)][0].astype(BF16)
-            to_pair(n).start()
-
-    def settle(g, j, extra, send):
-        n = 4 * g + j
-        to_pair(n).wait_recv()
-        for kind, i in extra:
-            along(kind, i).wait_recv()
+            z_out.at[n], z_in.at[n], sz_sem, rz_sem.at[n], device(parent[k] - k)
+        )
+
+    def along_other(k):
+        n = doubled.index(k)
+        return remote(
+            both_out.at[n], both_in.at[n], so_sem, ro_sem.at[n], device(parent[k] - k)
+        )
+
+    def prepare(k):
+        n = k % nz
+        for a in range(2):
+            terms[n, a] = own(at_z(-k), a).reshape(Y, feat, rows)
+            if k in doubled:
+                z_out[n, a] = terms[n, a, pl.ds(y, 1)][0].astype(BF16)
+                both_out[doubled.index(k), a] = terms[n, a, pl.ds(y_other, 1)][0].astype(BF16)
+        if k in doubled:
+            along(k).start()
+            along_other(k).start()
+
+    def hand(k):
+        n = k % nz
+        added = [c for c in children[k] if c in doubled]
+        for c in added:
+            along_other(c).wait_recv()
+        for a in range(2):
+            theirs = terms[n, a, pl.ds(y_other, 1)][0]
+            for c in added:
+                theirs = theirs + both_in[doubled.index(c), a].astype(F32)
+            pair_out[n, a] = theirs.astype(BF16)
+        to_pair(k).start()
+
+    def settle(k):
+        n = k % nz
+        to_pair(k).wait_recv()
+        for c in children[k]:
+            along(c).wait_recv()
         totals = []
         for a in range(2):
             total = terms[n, a, pl.ds(y, 1)][0] + pair_in[n, a].astype(F32)
-            for kind, i in extra:
-                total = total + z_in[kind, i, a].astype(F32)
-            if send:
-                z_out[j, g, a] = total.astype(BF16)
+            for c in children[k]:
+                total = total + z_in[c % nz, a].astype(F32)
+            if k != 0:
+                z_out[n, a] = total.astype(BF16)
             totals.append(total)
-        if send:
-            along(j, g).start()
+        if k != 0:
+            along(k).start()
         return totals
 
-    prepare(0)
+    def terms_of(level):
+        order = levels[level][::-1] if level == 0 else levels[level]
+        waits = [k for k in order if k in early]
+        for k in order:
+            prepare(k)
+            if k not in doubled and k not in waits:
+                hand(k)
+        for k in waits:
+            hand(k)
+
+    last = len(levels) - 1
+    terms_of(last)
     for o in range(1, n_dp):
         factors(o).start()
 
-    quad, place4 = z // 4, lax.rem(z, 4)
-
-    def sw_quads(k):
-        return remote(
-            sw_q.at[quad], sw_q.at[quad], swq_s.at[k - 1], swq_r.at[k - 1], device(4 * k)
-        )
-
-    def sw_near(k):
-        return remote(
-            sw_r.at[place4], sw_r.at[place4], swr_s.at[k], swr_r.at[k], device((1, -1, -2)[k])
-        )
+    def sw_send(c):
+        ref = sw_z.at[at_z(-parent[c])]
+        return remote(ref, ref, swz_s, swz_r.at[c % nz], device(c - parent[c]))
+
+    def sw_arrive(c):
+        ref = sw_z.at[at_z(-c)]
+        remote(ref, ref, swz_s, swz_r.at[c % nz], device(c - parent[c])).wait_recv()
 
     def sw_pair():
         return remote(sw_y.at[y], sw_y.at[y], swy_s, swy_r, pair)
@@ -415,52 +441,58 @@
         return remote(
             sw_all.at[e],
             sw_all.at[e],
-            swx_s.at[o - 1],
+            swx_s,
             swx_r.at[o - 1],
             {"expert": lax.rem(e + o, n_exp)},
         )
 
     line = dot_nt(jnp.ones((8, hidw), F32), hidden * hid_grad, lax.Precision.HIGHEST)
-    sw_q[pl.ds(quad, 1)] = line[None]
-    for k in range(1, groups):
-        sw_quads(k).start()
-
-    def sw_first():
-        for k in range(1, groups):
-            sw_quads(k).wait_recv()
-        total = sw_q[0]
-        for i in range(1, groups):
-            total = total + sw_q[i]
-        sw_r[pl.ds(place4, 1)] = total[None]
-        for k in range(3):
-            sw_near(k).start()
-
-    def sw_second():
-        for k in range(3):
-            sw_near(k).wait_recv()
-        sw_y[pl.ds(y, 1)] = (((sw_r[0] + sw_r[1]) + sw_r[2]) + sw_r[3])[None]
+    sw_z[pl.ds(z, 1)] = line[None]
+
+    def sw_level(level):
+        for k in levels[level]:
+            if level > 0:
+                sw_arrive(k)
+            for c in children[k]:
+                sw_send(c).start()
+
+    def sw_planes():
+        total = sw_z[0]
+        for i in range(1, nz):
+            total = total + sw_z[i]
+        sw_y[pl.ds(y, 1)] = total[None]
         sw_pair().start()
 
-    def sw_third():
+    def sw_experts():
         sw_pair().wait_recv()
         sw_all[pl.ds(e, 1)] = (sw_y[0] + sw_y[1])[None]
         for o in range(1, n_exp):
             sw_swap(o).start()
 
-    sw_stages = [sw_first, sw_second, sw_third]
-    for g in range(groups):
-        if g + 1 < groups:
-            prepare(g + 1)
-        settle(g, NEAR_DOWN, [], True)
-        settle(g, NEAR_UP, [], True)
-        settle(g, UP, [(UP, g - 1), (NEAR_UP, g - 1)] if g > 0 else [], True)
-        extra = [(NEAR_DOWN, g)] + ([(DOWN, g - 1)] if g > 0 else [])
-        if g < groups - 1:
-            settle(g, DOWN, extra, True)
-            if g > 0:
-                sw_stages.pop(0)()
-        else:
-            totals = settle(g, DOWN, extra + [(UP, g), (NEAR_UP, g)], False)
+    sw_level(0)
+    if last > 1:
+        terms_of(last - 1)
+    for k in levels[last]:
+        if k not in doubled:
+            settle(k)
+    sw_level(1)
+    for level in range(last - 1, 0, -1):
+        terms_of(level - 1)
+        for k in levels[level]:
+            if not children[k] and k not in doubled:
+                settle(k)
+        if level == 1:
+            sw_level(last)
+            sw_planes()
+        for k in levels[level]:
+            if children[k]:
+                settle(k)
+        if level > 1:
+            sw_level(last - level + 1)
+    if last == 1:
+        terms_of(0)
+        sw_planes()
+    totals = settle(0)
 
     back = eye(rows)
     for a in range(2):
@@ -469,8 +501,7 @@
     for o in range(1, n_exp):
         swap(out4, in4, s4_sem, r4_sem, o).start()
     in4[pl.ds(e, 1)] = out4[pl.ds(e, 1)]
-    for sw_stage in sw_stages:
-        sw_stage()
+    sw_experts()
 
     for o in range(1, n_dp):
         for p in range(planes):
@@ -506,6 +537,23 @@
     ]
     for store in stores[:3]:
         store.start()
+
+    def sent(ref, sem):
+        remote(ref, ref, sem, rg_sem.at[0], pair).wait_send()
+
+    count, singles = len(others), nz - len(doubled)
+    sent(out0.at[pl.ds(0, n_exp - 1)], s0_sem)
+    sent(xg.at[pl.ds(0, count), 0], sg_sem)
+    sent(xg.at[pl.ds(0, singles), 0], sy_sem)
+    sent(z_out.at[pl.ds(0, count)], sz_sem)
+    sent(pair_out.at[pl.ds(0, singles)], sp_sem)
+    if doubled:
+        sent(xg.at[pl.ds(0, len(doubled)), 0], sb_sem)
+        sent(both_out.at[pl.ds(0, len(doubled))], so_sem)
+    sent(sw_z.at[pl.ds(0, count)], swz_s)
+    sent(xq, xq_s)
+    sent(hq, hq_s)
+    sw_pair().wait_send()
 
     for o in range(1, n_exp):
         swap(out4, in4, s4_sem, r4_sem, o).wait_recv()
@@ -537,33 +585,8 @@
     logit_grad_ref[...] = jnp.where(which == 0, first, -first)
     stores[5].start()
 
-    for o in range(1, n_exp):
-        swap(out0, in0, s0_sem, r0_sem, o).wait_send()
-        swap(out4, in4, s4_sem, r4_sem, o).wait_send()
-        sw_swap(o).wait_send()
-    for i in range(groups):
-        step("chain_up", i).wait_send()
-        step("near_up", i).wait_send()
-        step("near_down", i).wait_send()
-        if i < groups - 1:
-            step("chain_down", i).wait_send()
-            step("both_down", i).wait_send()
-        for j in (NEAR_DOWN, NEAR_UP, UP, DOWN):
-            to_pair(4 * i + j).wait_send()
-            if j != DOWN or i < groups - 1:
-                along(j, i).wait_send()
-    for off in range(nz):
-        if off not in relayed:
-            across(off).wait_send()
-    for o in range(1, n_dp):
-        for p in range(planes):
-            quarter(o, p).wait_send()
-        factors(o).wait_send()
-    for k in range(1, groups):
-        sw_quads(k).wait_send()
-    for k in range(3):
-        sw_near(k).wait_send()
-    sw_pair().wait_send()
+    sent(out4.at[pl.ds(0, n_exp - 1)], s4_sem)
+    sent(sw_all.at[pl.ds(0, n_exp - 1)], swx_s)
     for store in stores:
         store.wait()
 
@@ -592,7 +615,6 @@
         hidw = gate_weight.shape[2]
         slot = tok // 2
         rows = n_exp * slot
-        groups = nz // 4
         planes = nz // n_dp
         pad = -(-feat // 128) * 128
         width = feat * n_t // n_dp
@@ -637,39 +659,42 @@
                 pltpu.VMEM((nz, 2, Y, feat, rows), F32),
                 pltpu.VMEM((nz,) + block, BF16),
                 pltpu.VMEM((nz,) + block, BF16),
-                pltpu.VMEM((4, groups) + block, BF16),
-                pltpu.VMEM((4, groups) + block, BF16),
-                pltpu.VMEM((groups, 8, rows), F32),
-                pltpu.VMEM((4, 8, rows), F32),
+                pltpu.VMEM((nz,) + block, BF16),
+                pltpu.VMEM((nz,) + block, BF16),
+                pltpu.VMEM((3,) + block, BF16),
+                pltpu.VMEM((3,) + block, BF16),
+                pltpu.VMEM((nz, 8, rows), F32),
                 pltpu.VMEM((Y, 8, rows), F32),
                 pltpu.VMEM((n_exp, 8, rows), F32),
                 pltpu.VMEM((n_exp, slot, 2 * pad), BF16),
                 pltpu.VMEM((n_exp, slot, 2 * pad), BF16),
                 dma((7,)),
                 dma((6,)),
+                dma,
                 dma((n_exp - 1,)),
+                dma,
+                dma((nz,)),
+                dma,
+                dma((nz,)),
+                dma,
+                dma((3,)),
+                dma,
+                dma((n_dp - 1, planes)),
+                dma,
+                dma((n_dp - 1,)),
+                dma,
+                dma((nz,)),
+                dma,
+                dma((nz,)),
+                dma,
+                dma((3,)),
+                dma,
+                dma((nz,)),
+                dma,
+                dma,
+                dma,
                 dma((n_exp - 1,)),
-                dma((nz,)),
-                dma((nz,)),
-                dma((5, groups)),
-                dma((5, groups)),
-                dma((n_dp - 1, planes)),
-                dma((n_dp - 1, planes)),
-                dma((n_dp - 1,)),
-                dma((n_dp - 1,)),
-                dma((nz,)),
-                dma((nz,)),
-                dma((4, groups)),
-                dma((4, groups)),
-                dma((max(groups - 1, 1),)),
-                dma((max(groups - 1, 1),)),
-                dma((3,)),
-                dma((3,)),
-                dma,
-                dma,
-                dma((n_exp - 1,)),
-                dma((n_exp - 1,)),
-                dma((n_exp - 1,)),
+                dma,
                 dma((n_exp - 1,)),
             ],
             compiler_params=pltpu.CompilerParams(

time: 86.1 us -> 83.4 us (0.969)
  Pallas kernels: 85.3 us -> 82.3 us
    pallas_call x1, Pallas kernels: 83.1 us -> 80.2 us  [on_device(): pl.pallas_call(functools.partial(kernel, (n_dp, n_exp, nz, tok, feat, hid...]
where the time goes in v3:
time: 83.4 us; the launch traced here: 82.9 us
  Pallas kernels  82.3 us (99%)
    pallas_call x1, Pallas kernels, on_device(): pl.pallas_call(functools.partial(kernel, (n_dp, n_exp, nz, tok, feat, hid...  80.2 us
    pallas_call x1, Pallas kernels, on_device(): pl.pallas_call(hand_over, out_shape=shapes, in_specs=[hbm] * 6, out_specs...  2.14 us

profile of v3, /device:TPU:1, one launch (start us, length us, event | category | flops | bytes accessed | tf_op | source)
XLA Modules:
  0.0 82.9 jit_solution(359975244890043517)
XLA Ops:
  0.6 80.2 %shard_map.118 = (bf16[32,96]{1,0:T(8,128)(2,1)}, bf16[32,96]{1,0:T(8,128)(2,1)}, f32[2,32]{1,0:T(2,128)}, bf16[768,256]{1,0:T(8,128)(2,1)}, bf16[768,256]{1,0:T(8,128)(2,1)}, /*index=5*/bf16[768,256]{1,0:T(8,128)(2,1)}) custom-call(bf16[32,96]{1,0:T(8,128)(2,1)} %tok_hbm.1, s32[2,32]{1,0:T(2,128)} %bitcast.12, f32[2,32]{1,0:T(2,128)} %bitcast.13, ...), custom_call_target="tpu_custom_call" | custom-call | tf_op jit(solution)/shard_map/pallas_call | solution.py:634
  80.8 2.1 %shard_map.119 = (bf16[32,96]{1,0:T(8,128)(2,1)}, bf16[32,96]{1,0:T(8,128)(2,1)}, f32[2,32]{1,0:T(2,128)}, bf16[768,256]{1,0:T(8,128)(2,1)}, bf16[768,256]{1,0:T(8,128)(2,1)}, /*index=5*/bf16[768,256]{1,0:T(8,128)(2,1)}) custom-call(bf16[32,96]{1,0:T(8,128)(2,1)} %get-tuple-element.18.refs_0_, bf16[32,96]{1,0:T(8,128)(2,1)} %get-tuple-element.19.refs_1_, ...), custom_call_target="tpu_custom_call" | custom-call | tf_op jit(solution)/shard_map/pallas_call | solution.py:704

commit v4 on v3

--- a/solution.py
+++ b/solution.py
@@ -35,19 +35,17 @@
 
 def tree(nz):
     groups = nz // 4
-    parent, levels, doubled = {}, [[0]], []
+    parent, levels = {}, [[0]]
     for i in range(groups):
         up, down = [2 * i + 2, 2 * i + 1], [-2 * i - 1]
         if i < groups - 1:
             down.insert(0, -2 * i - 2)
-        if i > 0 and i >= groups - 2:
-            doubled.append(-2 * i - 1)
-        if i > 0 and i == groups - 1:
-            doubled.append(2 * i + 1)
         parent.update({k: 2 * i for k in up})
         parent.update({k: -2 * i for k in down})
         levels.append([k for pair in zip(up, down) for k in pair] + up[len(down) :])
-    return parent, levels, tuple(doubled)
+    end = 2 * groups
+    doubled = [k for k in (3 - end, end - 1, 1 - end) if groups > 1 and parent[k] != 0]
+    return parent, levels, doubled, {end: 2 - end, end - 1: end - 2, 1 - end: 2 - end}
 
 
 def kernel(
@@ -129,8 +127,9 @@
     slot = tok // 2
     rows = n_exp * slot
     planes = nz // n_dp
-    parent, levels, doubled = tree(nz)
+    parent, levels, doubled, crossing = tree(nz)
     others = [k for level in levels[1:] for k in level]
+    cross = list(crossing)
     children = {
         k: sorted((c for c in others if parent[c] == k), key=lambda c: -abs(c - k))
         for k in [0] + others
@@ -144,14 +143,19 @@
     def at_z(off):
         return lax.rem(z + (off + nz), nz)
 
-    def device(off):
-        return {"tensor": at_z(off) * Y + y}
+    def device(off, other=False):
+        return {"tensor": at_z(off) * Y + (y_other if other else y)}
+
+    def crossed(c):
+        hop = c - crossing[c]
+        return hop - nz if hop > 2 else hop
 
     pair = {"tensor": z * Y + y_other}
 
     hops = {k - parent[k] for k in others}
     z_peers = sorted({h % nz for h in hops} | {-h % nz for h in hops})
     peers = [device(off) for off in z_peers] + [pair]
+    peers += [device(off, True) for off in z_peers]
     peers += [{"expert": lax.rem(e + o, n_exp)} for o in range(1, n_exp)]
     peers += [{"dp": lax.rem(d + o, n_dp)} for o in range(1, n_dp)]
     barrier = pltpu.get_barrier_semaphore()
@@ -225,13 +229,13 @@
 
     def swap(src, dst, send, recv, o):
         to = lax.rem(e + o, n_exp)
-        return remote(src.at[to], dst.at[e], send, recv.at[o - 1], {"expert": to})
+        return remote(src.at[to], dst.at[e], send, recv, {"expert": to})
 
     for o in range(1, n_exp):
         swap(out0, in0, s0_sem, r0_sem, o).start()
     in0[pl.ds(e, 1)] = out0[pl.ds(e, 1)]
-    for o in range(1, n_exp):
-        swap(out0, in0, s0_sem, r0_sem, o).wait_recv()
+    arrived = in0.at[pl.ds(0, n_exp - 1)]
+    remote(arrived, arrived, s0_sem, r0_sem, pair).wait_recv()
 
     unit = eye(pad)
     for a in range(2):
@@ -260,16 +264,6 @@
     def across(k):
         ref = xg.at[at_z(-k), y]
         return remote(ref, ref, sy_sem, ry_sem.at[k % nz], pair)
-
-    def quarter(o, p):
-        peer = lax.rem(d + o, n_dp)
-        return remote(
-            xg.at[peer * planes + p],
-            xq.at[o - 1, p],
-            xq_s,
-            xq_r.at[o - 1, p],
-            {"dp": peer},
-        )
 
     def complete(k):
         if k in doubled:
@@ -298,7 +292,7 @@
                 xg.at[block],
                 xq.at[o - 1, p],
                 xq_s,
-                xq_r.at[o - 1, p],
+                xq_r,
                 {"dp": peer},
             ).start()
 
@@ -311,17 +305,18 @@
             accumulate(at_z(-k))
             forward(at_z(-k))
 
+    last = len(levels) - 1
     for level, offsets in enumerate(levels):
         for k in offsets:
             if level > 0:
                 arrive(k)
-            far = [c for c in children[k] if abs(c - k) > 1]
-            for c in far:
-                deliver(c).start()
+            for c in children[k]:
+                if abs(c - k) > 1:
+                    deliver(c).start()
             if k not in doubled:
                 across(k).start()
             for c in children[k]:
-                if c not in far:
+                if abs(c - k) == 1:
                     deliver(c).start()
         if level == 0:
             for load in loads[4:]:
@@ -331,11 +326,11 @@
         for k in offsets:
             if k in early:
                 complete(k)
-    use(len(levels) - 1)
+    use(last)
 
     def factors(o):
         return remote(
-            hid, hq.at[o - 1], hq_s, hq_r.at[o - 1], {"dp": lax.rem(d + o, n_dp)}
+            hid, hq.at[o - 1], hq_s, hq_r, {"dp": lax.rem(d + o, n_dp)}
         )
 
     gate, lift, hid_grad = acc[0], acc[1], acc[2]
@@ -365,33 +360,27 @@
             z_out.at[n], z_in.at[n], sz_sem, rz_sem.at[n], device(parent[k] - k)
         )
 
-    def along_other(k):
-        n = doubled.index(k)
+    def along_across(k):
+        n = cross.index(k)
         return remote(
-            both_out.at[n], both_in.at[n], so_sem, ro_sem.at[n], device(parent[k] - k)
+            both_out.at[n], both_in.at[n], so_sem, ro_sem.at[n], device(-crossed(k), True)
         )
 
     def prepare(k):
         n = k % nz
         for a in range(2):
             terms[n, a] = own(at_z(-k), a).reshape(Y, feat, rows)
-            if k in doubled:
+            if k in crossing:
                 z_out[n, a] = terms[n, a, pl.ds(y, 1)][0].astype(BF16)
-                both_out[doubled.index(k), a] = terms[n, a, pl.ds(y_other, 1)][0].astype(BF16)
-        if k in doubled:
+                both_out[cross.index(k), a] = terms[n, a, pl.ds(y_other, 1)][0].astype(BF16)
+        if k in crossing:
             along(k).start()
-            along_other(k).start()
+            along_across(k).start()
 
     def hand(k):
         n = k % nz
-        added = [c for c in children[k] if c in doubled]
-        for c in added:
-            along_other(c).wait_recv()
         for a in range(2):
-            theirs = terms[n, a, pl.ds(y_other, 1)][0]
-            for c in added:
-                theirs = theirs + both_in[doubled.index(c), a].astype(F32)
-            pair_out[n, a] = theirs.astype(BF16)
+            pair_out[n, a] = terms[n, a, pl.ds(y_other, 1)][0].astype(BF16)
         to_pair(k).start()
 
     def settle(k):
@@ -399,11 +388,16 @@
         to_pair(k).wait_recv()
         for c in children[k]:
             along(c).wait_recv()
+        over = [c for c in cross if crossing[c] == k]
+        for c in over:
+            along_across(c).wait_recv()
         totals = []
         for a in range(2):
             total = terms[n, a, pl.ds(y, 1)][0] + pair_in[n, a].astype(F32)
             for c in children[k]:
                 total = total + z_in[c % nz, a].astype(F32)
+            for c in over:
+                total = total + both_in[cross.index(c), a].astype(F32)
             if k != 0:
                 z_out[n, a] = total.astype(BF16)
             totals.append(total)
@@ -411,28 +405,16 @@
             along(k).start()
         return totals
 
-    def terms_of(level):
-        order = levels[level][::-1] if level == 0 else levels[level]
-        waits = [k for k in order if k in early]
-        for k in order:
-            prepare(k)
-            if k not in doubled and k not in waits:
-                hand(k)
-        for k in waits:
-            hand(k)
-
-    last = len(levels) - 1
-    terms_of(last)
+    chain = [[k for k in level if children[k]] for level in levels]
+    near = [[k for k in level if not children[k]] for level in levels]
+    for k in levels[last]:
+        prepare(k)
     for o in range(1, n_dp):
         factors(o).start()
 
-    def sw_send(c):
-        ref = sw_z.at[at_z(-parent[c])]
-        return remote(ref, ref, swz_s, swz_r.at[c % nz], device(c - parent[c]))
-
-    def sw_arrive(c):
-        ref = sw_z.at[at_z(-c)]
-        remote(ref, ref, swz_s, swz_r.at[c % nz], device(c - parent[c])).wait_recv()
+    def sw_send(off):
+        ref = sw_z.at[z]
+        return remote(ref, ref, swz_s, swz_r, device(off))
 
     def sw_pair():
         return remote(sw_y.at[y], sw_y.at[y], swy_s, swy_r, pair)
@@ -442,21 +424,20 @@
             sw_all.at[e],
             sw_all.at[e],
             swx_s,
-            swx_r.at[o - 1],
+            swx_r,
             {"expert": lax.rem(e + o, n_exp)},
         )
 
     line = dot_nt(jnp.ones((8, hidw), F32), hidden * hid_grad, lax.Precision.HIGHEST)
     sw_z[pl.ds(z, 1)] = line[None]
 
-    def sw_level(level):
-        for k in levels[level]:
-            if level > 0:
-                sw_arrive(k)
-            for c in children[k]:
-                sw_send(c).start()
+    def sw_begin():
+        for off in range(1, nz):
+            sw_send(off).start()
 
     def sw_planes():
+        arrived = sw_z.at[pl.ds(0, nz - 1)]
+        remote(arrived, arrived, swz_s, swz_r, pair).wait_recv()
         total = sw_z[0]
         for i in range(1, nz):
             total = total + sw_z[i]
@@ -469,29 +450,21 @@
         for o in range(1, n_exp):
             sw_swap(o).start()
 
-    sw_level(0)
-    if last > 1:
-        terms_of(last - 1)
-    for k in levels[last]:
-        if k not in doubled:
+    for k in levels[last - 1]:
+        prepare(k)
+    for k in chain[last - 1]:
+        hand(k)
+    sw_begin()
+    for level in range(last - 1, 0, -1):
+        for k in near[level]:
+            hand(k)
+        for k in levels[level - 1]:
+            prepare(k)
+        for k in chain[level - 1]:
+            hand(k)
+        for k in chain[level] + near[level] if level == last - 1 else near[level] + chain[level]:
             settle(k)
-    sw_level(1)
-    for level in range(last - 1, 0, -1):
-        terms_of(level - 1)
-        for k in levels[level]:
-            if not children[k] and k not in doubled:
-                settle(k)
-        if level == 1:
-            sw_level(last)
-            sw_planes()
-        for k in levels[level]:
-            if children[k]:
-                settle(k)
-        if level > 1:
-            sw_level(last - level + 1)
-    if last == 1:
-        terms_of(0)
-        sw_planes()
+    sw_planes()
     totals = settle(0)
 
     back = eye(rows)
@@ -503,10 +476,8 @@
     in4[pl.ds(e, 1)] = out4[pl.ds(e, 1)]
     sw_experts()
 
-    for o in range(1, n_dp):
-        for p in range(planes):
-            quarter(o, p).wait_recv()
-        factors(o).wait_recv()
+    remote(xq, xq, xq_s, xq_r, pair).wait_recv()
+    remote(hq, hq, hq_s, hq_r, pair).wait_recv()
 
     @pl.loop(0, planes)
     def _(p):
@@ -541,22 +512,22 @@
     def sent(ref, sem):
         remote(ref, ref, sem, rg_sem.at[0], pair).wait_send()
 
-    count, singles = len(others), nz - len(doubled)
+    count, kept = len(others), nz - len(cross)
     sent(out0.at[pl.ds(0, n_exp - 1)], s0_sem)
     sent(xg.at[pl.ds(0, count), 0], sg_sem)
-    sent(xg.at[pl.ds(0, singles), 0], sy_sem)
-    sent(z_out.at[pl.ds(0, count)], sz_sem)
-    sent(pair_out.at[pl.ds(0, singles)], sp_sem)
+    sent(xg.at[pl.ds(0, nz - len(doubled)), 0], sy_sem)
     if doubled:
         sent(xg.at[pl.ds(0, len(doubled)), 0], sb_sem)
-        sent(both_out.at[pl.ds(0, len(doubled))], so_sem)
-    sent(sw_z.at[pl.ds(0, count)], swz_s)
+    sent(z_out.at[pl.ds(0, count)], sz_sem)
+    sent(pair_out.at[pl.ds(0, kept)], sp_sem)
+    sent(both_out, so_sem)
+    sent(sw_z.at[pl.ds(0, nz - 1)], swz_s)
     sent(xq, xq_s)
     sent(hq, hq_s)
     sw_pair().wait_send()
 
-    for o in range(1, n_exp):
-        swap(out4, in4, s4_sem, r4_sem, o).wait_recv()
+    arrived = in4.at[pl.ds(0, n_exp - 1)]
+    remote(arrived, arrived, s4_sem, r4_sem, pair).wait_recv()
     came = in4[...].reshape(rows, 2 * pad)
     picked = [dot(s, came) for s in select]
     mixed_ref[...] = (
@@ -567,8 +538,8 @@
     ).astype(BF16)
     for store in stores[3:5]:
         store.start()
-    for o in range(1, n_exp):
-        sw_swap(o).wait_recv()
+    arrived = sw_all.at[pl.ds(0, n_exp - 1)]
+    remote(arrived, arrived, swx_s, swx_r, pair).wait_recv()
     sw = []
     for k in range(2):
         line = jnp.zeros((tok, rows), F32)
@@ -671,7 +642,7 @@
                 dma((7,)),
                 dma((6,)),
                 dma,
-                dma((n_exp - 1,)),
+                dma,
                 dma,
                 dma((nz,)),
                 dma,
@@ -679,9 +650,9 @@
                 dma,
                 dma((3,)),
                 dma,
-                dma((n_dp - 1, planes)),
-                dma,
-                dma((n_dp - 1,)),
+                dma,
+                dma,
+                dma,
                 dma,
                 dma((nz,)),
                 dma,
@@ -689,13 +660,13 @@
                 dma,
                 dma((3,)),
                 dma,
-                dma((nz,)),
-                dma,
-                dma,
-                dma,
-                dma((n_exp - 1,)),
-                dma,
-                dma((n_exp - 1,)),
+                dma,
+                dma,
+                dma,
+                dma,
+                dma,
+                dma,
+                dma,
             ],
             compiler_params=pltpu.CompilerParams(
                 collective_id=0, has_side_effects=True, vmem_limit_bytes=60 * 1024 * 1024

time: 83.4 us -> 83.8 us (level)
  no operation moved by 1% of the time
where the time goes in v4:
time: 83.8 us; the launch traced here: 83.6 us
  Pallas kernels  82.9 us (99%)
    pallas_call x1, Pallas kernels, on_device(): pl.pallas_call(functools.partial(kernel, (n_dp, n_exp, nz, tok, feat, hid...  80.8 us
    pallas_call x1, Pallas kernels, on_device(): pl.pallas_call(hand_over, out_shape=shapes, in_specs=[hbm] * 6, out_specs...  2.14 us

profile of v4, /device:TPU:1, one launch (start us, length us, event | category | flops | bytes accessed | tf_op | source)
XLA Modules:
  0.0 83.6 jit_solution(15442516818578195464)
XLA Ops:
  0.6 80.8 %shard_map.118 = (bf16[32,96]{1,0:T(8,128)(2,1)}, bf16[32,96]{1,0:T(8,128)(2,1)}, f32[2,32]{1,0:T(2,128)}, bf16[768,256]{1,0:T(8,128)(2,1)}, bf16[768,256]{1,0:T(8,128)(2,1)}, /*index=5*/bf16[768,256]{1,0:T(8,128)(2,1)}) custom-call(bf16[32,96]{1,0:T(8,128)(2,1)} %tok_hbm.1, s32[2,32]{1,0:T(2,128)} %bitcast.12, f32[2,32]{1,0:T(2,128)} %bitcast.13, ...), custom_call_target="tpu_custom_call" | custom-call | tf_op jit(solution)/shard_map/pallas_call | solution.py:605
  81.4 2.1 %shard_map.119 = (bf16[32,96]{1,0:T(8,128)(2,1)}, bf16[32,96]{1,0:T(8,128)(2,1)}, f32[2,32]{1,0:T(2,128)}, bf16[768,256]{1,0:T(8,128)(2,1)}, bf16[768,256]{1,0:T(8,128)(2,1)}, /*index=5*/bf16[768,256]{1,0:T(8,128)(2,1)}) custom-call(bf16[32,96]{1,0:T(8,128)(2,1)} %get-tuple-element.18.refs_0_, bf16[32,96]{1,0:T(8,128)(2,1)} %get-tuple-element.19.refs_1_, ...), custom_call_target="tpu_custom_call" | custom-call | tf_op jit(solution)/shard_map/pallas_call | solution.py:675

commit v5 on v4

--- a/solution.py
+++ b/solution.py
@@ -57,20 +57,16 @@
     wu_hbm,
     wd_hbm,
     og_hbm,
-    mixed_hbm,
-    in_grad_hbm,
-    logit_grad_hbm,
-    gate_grad_hbm,
-    up_grad_hbm,
-    down_grad_hbm,
+    mixed_ref,
+    in_grad_ref,
+    logit_grad_ref,
+    gate_grad_ref,
+    up_grad_ref,
+    down_grad_ref,
     tok_ref,
     ids_ref,
     logit_ref,
     og_ref,
-    mixed_ref,
-    in_grad_ref,
-    logit_grad_ref,
-    grads_ref,
     wg,
     wu,
     wd,
@@ -95,7 +91,6 @@
     out4,
     in4,
     load_sem,
-    store_sem,
     s0_sem,
     r0_sem,
     sy_sem,
@@ -486,28 +481,12 @@
         ]
         parts = [hid] + [hq.at[o] for o in range(n_dp - 1)]
         here = pl.ds(pl.multiple_of(p * Y * feat, Y * feat), Y * feat)
-        for n, a, i in ((0, 0, 1), (1, 0, 2), (2, 1, 0)):
+        for ref, a, i in ((gate_grad_ref, 0, 1), (up_grad_ref, 0, 2), (down_grad_ref, 1, 0)):
             total = None
             for b, h in zip(both, parts):
                 term = dot(b[:, a].reshape(Y * feat, rows), h[:, i * hidw : (i + 1) * hidw])
                 total = term if total is None else total + term
-            grads_ref[n, here, :] = total.astype(BF16)
-
-    stores = [
-        pltpu.make_async_copy(src, dst, store_sem.at[i])
-        for i, (src, dst) in enumerate(
-            (
-                (grads_ref.at[0], gate_grad_hbm),
-                (grads_ref.at[1], up_grad_hbm),
-                (grads_ref.at[2], down_grad_hbm),
-                (mixed_ref, mixed_hbm),
-                (in_grad_ref, in_grad_hbm),
-                (logit_grad_ref, logit_grad_hbm),
-            )
-        )
-    ]
-    for store in stores[:3]:
-        store.start()
+            ref[here, :] = total.astype(BF16)
 
     def sent(ref, sem):
         remote(ref, ref, sem, rg_sem.at[0], pair).wait_send()
@@ -536,8 +515,6 @@
     in_grad_ref[...] = (
         picked[0][:, pad : pad + feat] + picked[1][:, pad : pad + feat]
     ).astype(BF16)
-    for store in stores[3:5]:
-        store.start()
     arrived = sw_all.at[pl.ds(0, n_exp - 1)]
     remote(arrived, arrived, swx_s, swx_r, pair).wait_recv()
     sw = []
@@ -554,26 +531,20 @@
     )
     which = lax.broadcasted_iota(jnp.int32, (2, tok), 0)
     logit_grad_ref[...] = jnp.where(which == 0, first, -first)
-    stores[5].start()
 
     sent(out4.at[pl.ds(0, n_exp - 1)], s4_sem)
     sent(sw_all.at[pl.ds(0, n_exp - 1)], swx_s)
-    for store in stores:
-        store.wait()
 
 
 def hand_over(*refs):
-    count = (len(refs) - 2) // 3
-    sources, results, held = refs[:count], refs[count : 2 * count], refs[2 * count : 3 * count]
-    in_sem, out_sem = refs[-2:]
-    ins = [pltpu.make_async_copy(sources[i], held[i], in_sem.at[i]) for i in range(count)]
-    outs = [pltpu.make_async_copy(held[i], results[i], out_sem.at[i]) for i in range(count)]
-    for copy in ins:
+    count = len(refs) // 2
+    sem = refs[-1]
+    copies = [
+        pltpu.make_async_copy(refs[i], refs[count + i], sem.at[i]) for i in range(count)
+    ]
+    for copy in copies:
         copy.start()
-    for before, after in zip(ins, outs):
-        before.wait()
-        after.start()
-    for copy in outs:
+    for copy in copies:
         copy.wait()
 
 
@@ -590,6 +561,7 @@
         pad = -(-feat // 128) * 128
         width = feat * n_t // n_dp
         hbm = pl.BlockSpec(memory_space=pl.ANY)
+        vmem = pl.BlockSpec(memory_space=pltpu.VMEM)
         dma = pltpu.SemaphoreType.DMA
         weights = [w.reshape(nz, Y * feat, hidw) for w in (gate_weight, up_weight, down_weight)]
         grad = jax.ShapeDtypeStruct((width, hidw), BF16)
@@ -604,18 +576,14 @@
         block = (2, feat, rows)
         outs = pl.pallas_call(
             functools.partial(kernel, (n_dp, n_exp, nz, tok, feat, hidw, pad)),
-            out_shape=shapes,
+            out_shape=tuple(pltpu.VMEM(out.shape, out.dtype) for out in shapes),
             in_specs=[hbm] * 7,
-            out_specs=[hbm] * 6,
+            out_specs=[vmem] * 6,
             scratch_shapes=[
                 pltpu.VMEM((tok, feat), BF16),
                 pltpu.VMEM((2, tok), jnp.int32),
                 pltpu.VMEM((2, tok), F32),
                 pltpu.VMEM((tok, feat), BF16),
-                pltpu.VMEM((tok, feat), BF16),
-                pltpu.VMEM((tok, feat), BF16),
-                pltpu.VMEM((2, tok), F32),
-                pltpu.VMEM((3, width, hidw), BF16),
                 pltpu.VMEM((nz, Y * feat, hidw), BF16),
                 pltpu.VMEM((nz, Y * feat, hidw), BF16),
                 pltpu.VMEM((nz, Y * feat, hidw), BF16),
@@ -640,7 +608,6 @@
                 pltpu.VMEM((n_exp, slot, 2 * pad), BF16),
                 pltpu.VMEM((n_exp, slot, 2 * pad), BF16),
                 dma((7,)),
-                dma((6,)),
                 dma,
                 dma,
                 dma,
@@ -675,11 +642,10 @@
         mixed, in_grad, logit_grad, gate_grad, up_grad, down_grad = pl.pallas_call(
             hand_over,
             out_shape=shapes,
-            in_specs=[hbm] * 6,
+            in_specs=[vmem] * 6,
             out_specs=[hbm] * 6,
-            scratch_shapes=[pltpu.VMEM(out.shape, out.dtype) for out in shapes]
-            + [dma((6,)), dma((6,))],
-            compiler_params=pltpu.CompilerParams(vmem_limit_bytes=60 * 1024 * 1024),
+            scratch_shapes=[dma((6,))],
+            compiler_params=pltpu.CompilerParams(vmem_limit_bytes=4 * 1024 * 1024),
         )(*outs)
         return mixed, in_grad, logit_grad.T, gate_grad[None], up_grad[None], down_grad[None]
 

time: 83.8 us -> 82 us (0.979)
  Pallas kernels: 82.9 us -> 81.2 us
    pallas_call x1, Pallas kernels: 2.14 us -> 1.07 us  [on_device(): pl.pallas_call(hand_over, out_shape=shapes, in_specs=[vmem] * 6, out_spec...]
where the time goes in v5:
time: 82 us; the launch traced here: 81.9 us
  Pallas kernels  81.2 us (99%)
    pallas_call x1, Pallas kernels, on_device(): pl.pallas_call(functools.partial(kernel, (n_dp, n_exp, nz, tok, feat, hid...  80.2 us

profile of v5, /device:TPU:1, one launch (start us, length us, event | category | flops | bytes accessed | tf_op | source)
XLA Modules:
  0.0 81.9 jit_solution(8358439612236073605)
XLA Ops:
  0.6 80.2 %shard_map.118 = (bf16[32,96]{1,0:T(8,128)(2,1)S(1)}, bf16[32,96]{1,0:T(8,128)(2,1)S(1)}, f32[2,32]{1,0:T(2,128)S(1)}, bf16[768,256]{1,0:T(8,128)(2,1)S(1)}, bf1...) custom-call(bf16[32,96]{1,0:T(8,128)(2,1)} %tok_hbm.1, s32[2,32]{1,0:T(2,128)} %bitcast.12, f32[2,32]{1,0:T(2,128)} %bitcast.13, ...), custom_call_target="tpu_custom_call" | custom-call | tf_op jit(solution)/shard_map/pallas_call | solution.py:577
  80.8 1.1 %shard_map.119 = (bf16[32,96]{1,0:T(8,128)(2,1)}, bf16[32,96]{1,0:T(8,128)(2,1)}, f32[2,32]{1,0:T(2,128)}, bf16[768,256]{1,0:T(8,128)(2,1)}, bf16[768,256]{1,0:T(8,128)(2,1)}, /*index=5*/bf16[768,256]{1,0:T(8,128)(2,1)}) custom-call(bf16[32,96]{1,0:T(8,128)(2,1)S(1)} %get-tuple-element.18.refs_0_, bf16[32,96]{1,0:T(8,128)(2,1)S(1)} %get-tuple-element.19.refs_1_, ...), custom_call_target="tpu_custom_call" | custom-call | tf_op jit(solution)/shard_map/pallas_call | solution.py:642

commit v6 on v5

--- a/solution.py
+++ b/solution.py
@@ -45,7 +45,7 @@
         levels.append([k for pair in zip(up, down) for k in pair] + up[len(down) :])
     end = 2 * groups
     doubled = [k for k in (3 - end, end - 1, 1 - end) if groups > 1 and parent[k] != 0]
-    return parent, levels, doubled, {end: 2 - end, end - 1: end - 2, 1 - end: 2 - end}
+    return parent, levels, doubled
 
 
 def kernel(
@@ -83,8 +83,6 @@
     pair_in,
     z_out,
     z_in,
-    both_out,
-    both_in,
     sw_z,
     sw_y,
     sw_all,
@@ -107,8 +105,6 @@
     rp_sem,
     sz_sem,
     rz_sem,
-    so_sem,
-    ro_sem,
     swz_s,
     swz_r,
     swy_s,
@@ -122,9 +118,8 @@
     slot = tok // 2
     rows = n_exp * slot
     planes = nz // n_dp
-    parent, levels, doubled, crossing = tree(nz)
+    parent, levels, doubled = tree(nz)
     others = [k for level in levels[1:] for k in level]
-    cross = list(crossing)
     children = {
         k: sorted((c for c in others if parent[c] == k), key=lambda c: -abs(c - k))
         for k in [0] + others
@@ -138,19 +133,14 @@
     def at_z(off):
         return lax.rem(z + (off + nz), nz)
 
-    def device(off, other=False):
-        return {"tensor": at_z(off) * Y + (y_other if other else y)}
-
-    def crossed(c):
-        hop = c - crossing[c]
-        return hop - nz if hop > 2 else hop
+    def device(off):
+        return {"tensor": at_z(off) * Y + y}
 
     pair = {"tensor": z * Y + y_other}
 
     hops = {k - parent[k] for k in others}
     z_peers = sorted({h % nz for h in hops} | {-h % nz for h in hops})
     peers = [device(off) for off in z_peers] + [pair]
-    peers += [device(off, True) for off in z_peers]
     peers += [{"expert": lax.rem(e + o, n_exp)} for o in range(1, n_exp)]
     peers += [{"dp": lax.rem(d + o, n_dp)} for o in range(1, n_dp)]
     barrier = pltpu.get_barrier_semaphore()
@@ -355,23 +345,10 @@
             z_out.at[n], z_in.at[n], sz_sem, rz_sem.at[n], device(parent[k] - k)
         )
 
-    def along_across(k):
-        n = cross.index(k)
-        return remote(
-            both_out.at[n], both_in.at[n], so_sem, ro_sem.at[n], device(-crossed(k), True)
-        )
-
     def prepare(k):
         n = k % nz
         for a in range(2):
             terms[n, a] = own(at_z(-k), a).reshape(Y, feat, rows)
-            if k in crossing:
-                z_out[n, a] = terms[n, a, pl.ds(y, 1)][0].astype(BF16)
-                both_out[cross.index(k), a] = terms[n, a, pl.ds(y_other, 1)][0].astype(BF16)
-        if k in crossing:
-            along(k).start()
-            along_across(k).start()
-
     def hand(k):
         n = k % nz
         for a in range(2):
@@ -383,16 +360,11 @@
         to_pair(k).wait_recv()
         for c in children[k]:
             along(c).wait_recv()
-        over = [c for c in cross if crossing[c] == k]
-        for c in over:
-            along_across(c).wait_recv()
         totals = []
         for a in range(2):
             total = terms[n, a, pl.ds(y, 1)][0] + pair_in[n, a].astype(F32)
             for c in children[k]:
                 total = total + z_in[c % nz, a].astype(F32)
-            for c in over:
-                total = total + both_in[cross.index(c), a].astype(F32)
             if k != 0:
                 z_out[n, a] = total.astype(BF16)
             totals.append(total)
@@ -404,6 +376,7 @@
     near = [[k for k in level if not children[k]] for level in levels]
     for k in levels[last]:
         prepare(k)
+        hand(k)
     for o in range(1, n_dp):
         factors(o).start()
 
@@ -449,15 +422,17 @@
         prepare(k)
     for k in chain[last - 1]:
         hand(k)
+    for k in levels[last]:
+        settle(k)
     sw_begin()
+    for k in near[last - 1]:
+        hand(k)
     for level in range(last - 1, 0, -1):
-        for k in near[level]:
-            hand(k)
         for k in levels[level - 1]:
             prepare(k)
-        for k in chain[level - 1]:
+        for k in chain[level - 1] + near[level - 1]:
             hand(k)
-        for k in chain[level] + near[level] if level == last - 1 else near[level] + chain[level]:
+        for k in near[level] + chain[level]:
             settle(k)
     sw_planes()
     totals = settle(0)
@@ -491,15 +466,14 @@
     def sent(ref, sem):
         remote(ref, ref, sem, rg_sem.at[0], pair).wait_send()
 
-    count, kept = len(others), nz - len(cross)
+    count = len(others)
     sent(out0.at[pl.ds(0, n_exp - 1)], s0_sem)
     sent(xg.at[pl.ds(0, count), 0], sg_sem)
     sent(xg.at[pl.ds(0, nz - len(doubled)), 0], sy_sem)
     if doubled:
         sent(xg.at[pl.ds(0, len(doubled)), 0], sb_sem)
     sent(z_out.at[pl.ds(0, count)], sz_sem)
-    sent(pair_out.at[pl.ds(0, kept)], sp_sem)
-    sent(both_out, so_sem)
+    sent(pair_out, sp_sem)
     sent(sw_z.at[pl.ds(0, nz - 1)], swz_s)
     sent(xq, xq_s)
     sent(hq, hq_s)
@@ -600,8 +574,6 @@
                 pltpu.VMEM((nz,) + block, BF16),
                 pltpu.VMEM((nz,) + block, BF16),
                 pltpu.VMEM((nz,) + block, BF16),
-                pltpu.VMEM((3,) + block, BF16),
-                pltpu.VMEM((3,) + block, BF16),
                 pltpu.VMEM((nz, 8, rows), F32),
                 pltpu.VMEM((Y, 8, rows), F32),
                 pltpu.VMEM((n_exp, 8, rows), F32),
@@ -624,8 +596,6 @@
                 dma((nz,)),
                 dma,
                 dma((nz,)),
-                dma,
-                dma((3,)),
                 dma,
                 dma,
                 dma,

time: 82 us -> 80.6 us (0.983)
  Pallas kernels: 81.2 us -> 79.7 us
    pallas_call x1, Pallas kernels: 80.2 us -> 78.6 us  [on_device(): pl.pallas_call(functools.partial(kernel, (n_dp, n_exp, nz, tok, feat, hid...]
where the time goes in v6:
time: 80.6 us; the launch traced here: 80.4 us
  Pallas kernels  79.7 us (99%)
    pallas_call x1, Pallas kernels, on_device(): pl.pallas_call(functools.partial(kernel, (n_dp, n_exp, nz, tok, feat, hid...  78.6 us

profile of v6, /device:TPU:1, one launch (start us, length us, event | category | flops | bytes accessed | tf_op | source)
XLA Modules:
  0.0 80.4 jit_solution(15545823883355058528)
XLA Ops:
  0.6 78.6 %shard_map.118 = (bf16[32,96]{1,0:T(8,128)(2,1)S(1)}, bf16[32,96]{1,0:T(8,128)(2,1)S(1)}, f32[2,32]{1,0:T(2,128)S(1)}, bf16[768,256]{1,0:T(8,128)(2,1)S(1)}, bf1...) custom-call(bf16[32,96]{1,0:T(8,128)(2,1)} %tok_hbm.1, s32[2,32]{1,0:T(2,128)} %bitcast.12, f32[2,32]{1,0:T(2,128)} %bitcast.13, ...), custom_call_target="tpu_custom_call" | custom-call | tf_op jit(solution)/shard_map/pallas_call | solution.py:551
  79.3 1.1 %shard_map.119 = (bf16[32,96]{1,0:T(8,128)(2,1)}, bf16[32,96]{1,0:T(8,128)(2,1)}, f32[2,32]{1,0:T(2,128)}, bf16[768,256]{1,0:T(8,128)(2,1)}, bf16[768,256]{1,0:T(8,128)(2,1)}, /*index=5*/bf16[768,256]{1,0:T(8,128)(2,1)}) custom-call(bf16[32,96]{1,0:T(8,128)(2,1)S(1)} %get-tuple-element.18.refs_0_, bf16[32,96]{1,0:T(8,128)(2,1)S(1)} %get-tuple-element.19.refs_1_, ...), custom_call_target="tpu_custom_call" | custom-call | tf_op jit(solution)/shard_map/pallas_call | solution.py:612
